TPU v7x, 32 devices: a whole 2x2x4 slice. The times are simulated.
32 devices in a mesh: groups: 2 (over y), tm: 4 (over z), zoom: 2 (over x), pol: 2 (over core).
Axes of the slice: x: 2, y: 2, z: 4, core: 2. Of those that a mesh axis runs over, the one named last changes fastest.
Arguments:
- voltages: bfloat16 [2, 4, 7464960], P('pol', 'groups', ('tm', 'zoom')), parts along dimension 1, may hold values from -6 to 6
- section1_taps: float32 [12, 512], replicated, may hold values from -0.078125 to 0.078125
- section2_taps: float32 [5, 3456], replicated, may hold values from -0.046875 to 0.046875
- band_starts: int32 [4], P('groups'), parts along dimension 0, may hold values from 0 to 511
- band_widths: int32 [4], P('groups'), parts along dimension 0, may hold values from 1 to 20, 24 in all
Outputs:
- fine: float32 [2, 2, 4, 1, 58320], P('pol', 'zoom', 'groups', None, 'tm'), parts along dimension 2
There are 2 independent parts, one for each index of `groups`. A program takes and returns all parts, laid end to end along the dimension named above; an argument that names none is the same for every part. Nothing has to cross between parts.
Inputs may be any that keep to these rules, and one draw needn't show every extreme that they name: `band_widths`: the 2 widths sum to 24, and one band has exactly 20 coarse channels.
All inputs are finite; a program needn't handle non-finite values.
Results may differ from a plain program's by a relative error of at most 0.0069.
Values may be sent and summed in bfloat16 or wider, within the bound.
No kernel may reach another device: no remote copies, remote signals or barrier semaphores. Data moves between devices by JAX's collectives and lax.ppermute only.
A program may use at most 192 MiB of HBM per device.

v0:
```python
import math

import jax
import jax.numpy as jnp
import numpy as np
from jax import lax
from jax.sharding import PartitionSpec as P

HOP = 432
FA = 27
FB = 128
KEEP = 2916
EDGE = 128
CH_DEV = 5
LIVE_DEV = 3


def shifted(value, axis, steps):
    count = lax.axis_size(axis)
    initial, last = (max(0, -steps), min(count, count - steps))
    return lax.ppermute(value, axis, [(source, source + steps) for source in range(initial, last)])


def with_halo(value, sides, width):
    for axis, dim in sides:
        count, length = (lax.axis_size(axis), value.shape[dim])
        up = [(i, (i + 1) % count) for i in range(count - 1)]
        down = [(j, i) for i, j in up]
        last = lax.slice_in_dim(value, length - width, length, axis=dim)
        initial = lax.slice_in_dim(value, 0, width, axis=dim)
        before = lax.ppermute(last, axis, up)
        after = lax.ppermute(initial, axis, down)
        value = jnp.concatenate([before, value, after], axis=dim)
    return value


def angle_table(rows, cols, length):
    product = (
        jnp.arange(rows, dtype=jnp.int32)[:, None]
        * jnp.arange(cols, dtype=jnp.int32)[None, :]
        % length
    )
    return product.astype(jnp.float32) * (2.0 * math.pi / length)


def rotation_block(length):
    angles = angle_table(length, length, length)
    cosine_tab = jnp.cos(angles).astype(jnp.bfloat16)
    sine_tab = jnp.sin(angles).astype(jnp.bfloat16)
    return jnp.stack([jnp.stack([cosine_tab, sine_tab]), jnp.stack([-sine_tab, cosine_tab])])


def joined_table(length):
    angles = angle_table(length, length, length)
    cosine_tab = jnp.cos(angles).astype(jnp.bfloat16)
    sine_tab = jnp.sin(angles).astype(jnp.bfloat16)
    top_rows = jnp.concatenate([cosine_tab, -sine_tab], axis=1)
    bottom_rows = jnp.concatenate([sine_tab, cosine_tab], axis=1)
    return jnp.concatenate([top_rows, bottom_rows], axis=0)


def bin_index(radix_a, radix_b, keep_len, edge_len):
    fine_len = radix_a * radix_b
    offsets = (np.arange(keep_len + 2 * edge_len) - keep_len // 2 - edge_len) % fine_len
    base = offsets % radix_a * (2 * radix_b) + offsets // radix_a
    return (base, base + radix_b)


def frame_view(segment, spectra, chan_len, hop_len):
    pieces = -(-chan_len // hop_len)
    framed = segment[:, : (spectra + pieces - 1) * hop_len].reshape(
        segment.shape[0], spectra + pieces - 1, hop_len
    )
    joined = jnp.concatenate(
        [framed[:, offset : offset + spectra] for offset in range(pieces)], axis=2
    )
    return joined[:, :, :chan_len]


def weighted_frames(signal, taps, spectra, hop_len):
    chan_len = taps.shape[1]
    running = jnp.zeros((2, spectra, chan_len), jnp.float32)
    for tap_index in range(taps.shape[0]):
        frames = frame_view(signal[:, tap_index * chan_len :], spectra, chan_len, hop_len)
        running = running + taps[tap_index][None, None, :] * frames.astype(jnp.float32)
    return running.astype(jnp.bfloat16)


def fine_spectra(series, section2_taps, radix_a, radix_b, keep_len, edge_len):
    tap_count, fine_len = section2_taps.shape
    items = series.shape[1]
    row_count = series.shape[2] // fine_len
    spectra = row_count - tap_count + 1
    row_blocks = series.reshape(2, items, row_count, fine_len)
    running = jnp.zeros((2, items, spectra, fine_len), jnp.float32)
    for tap_index in range(tap_count):
        running = running + section2_taps[tap_index] * row_blocks[
            :, :, tap_index : tap_index + spectra
        ].astype(jnp.float32)
    weighted = running.astype(jnp.bfloat16).reshape(2, items, spectra, radix_a, radix_b)
    partial_value = jnp.einsum(
        "pqkm,qcfmb->pcfkb", rotation_block(radix_a), weighted, preferred_element_type=jnp.float32
    )
    angles = angle_table(radix_a, radix_b, fine_len)
    cosine_tab = jnp.cos(angles)
    sine_tab = jnp.sin(angles)
    real_part = partial_value[0] * cosine_tab + partial_value[1] * sine_tab
    imag_part = partial_value[1] * cosine_tab - partial_value[0] * sine_tab
    twiddled = jnp.concatenate([real_part, imag_part], axis=-1).astype(jnp.bfloat16)
    spectrum = jnp.einsum(
        "cfkm,mj->cfkj", twiddled, joined_table(radix_b), preferred_element_type=jnp.float32
    )
    flattened = spectrum.reshape(items, spectra, radix_a * 2 * radix_b)
    real_index, imag_index = bin_index(radix_a, radix_b, keep_len, edge_len)
    return jnp.stack(
        [jnp.take(flattened, real_index, axis=2), jnp.take(flattened, imag_index, axis=2)]
    )


def stitch_bands(extended, upper_rim, lower_rim, slot_ids, band_width, keep_len, edge_len):
    centre = extended[..., edge_len : edge_len + keep_len]
    live = (slot_ids < band_width).astype(jnp.float32)[None, :, None, None]
    upper_ok = (slot_ids + 1 < band_width).astype(jnp.float32)[None, :, None, None]
    lower_ok = ((slot_ids >= 1) & (slot_ids < band_width)).astype(jnp.float32)[None, :, None, None]
    ramp = (jnp.arange(edge_len, dtype=jnp.float32) + 0.5) / (2.0 * edge_len)
    upper_weight = ramp * upper_ok
    lower_weight = ramp[::-1] * lower_ok
    low_part = centre[..., :edge_len] * (1.0 - lower_weight) + lower_rim * lower_weight
    high_part = centre[..., keep_len - edge_len :] * (1.0 - upper_weight) + upper_rim * upper_weight
    joined = jnp.concatenate(
        [low_part, centre[..., edge_len : keep_len - edge_len], high_part], axis=-1
    )
    return joined * live


def on_device(voltages, section1_taps, section2_taps, band_starts, band_widths):
    signal = voltages[0]
    tap_count, chan_len = section1_taps.shape
    spectra = signal.shape[1] // HOP
    rim_len = tap_count * chan_len - HOP
    pieces = -(-chan_len // HOP)
    following = shifted(signal[:, :rim_len], ("tm", "zoom"), -1)
    padded = jnp.concatenate(
        [signal, following, jnp.zeros((2, pieces * HOP), jnp.bfloat16)], axis=1
    )
    weighted = weighted_frames(padded, section1_taps, spectra, HOP)
    coarse = jnp.einsum(
        "pqkn,qsn->pks", rotation_block(chan_len), weighted, preferred_element_type=jnp.float32
    ).astype(jnp.bfloat16)
    tm_count = lax.axis_size("tm")
    zoom_count = lax.axis_size("zoom")
    slot_local = jnp.arange(CH_DEV, dtype=jnp.int32)
    slot_ids = lax.axis_index("tm") * CH_DEV + slot_local
    band_count = band_widths.shape[0]
    band_ids = jnp.arange(band_count, dtype=jnp.int32)
    my_band = band_ids == lax.axis_index("zoom")
    band_width = jnp.sum(jnp.where(my_band, band_widths, 0))
    device_count = tm_count * zoom_count
    live_count = LIVE_DEV * device_count
    band_ends = jnp.cumsum(band_widths)
    band_firsts = band_ends - band_widths
    live_ids = jnp.arange(live_count, dtype=jnp.int32)
    band_of = jnp.sum((band_ends[None, :] <= live_ids[:, None]).astype(jnp.int32), axis=1)
    member = band_of[:, None] == band_ids[None, :]
    first_of = jnp.sum(jnp.where(member, band_firsts[None, :], 0), axis=1)
    start_of = jnp.sum(jnp.where(member, band_starts[None, :], 0), axis=1)
    live_channels = (start_of + live_ids - first_of) % chan_len
    packed_order = live_channels.reshape(device_count, LIVE_DEV).T.reshape(-1)
    packed = jnp.take(coarse, packed_order, axis=1).reshape(2, LIVE_DEV, device_count, spectra)
    received = lax.all_to_all(packed, ("tm", "zoom"), split_axis=2, concat_axis=2, tiled=True)
    series = received.reshape(2, received.shape[1], -1)
    computed = fine_spectra(series, section2_taps, FA, FB, KEEP, EDGE)
    wanted = jnp.sum(jnp.where(my_band, band_firsts, 0)) + slot_ids
    valid = slot_ids < band_width
    piece = lax.all_gather(computed, ("tm", "zoom"), axis=1, tiled=True)
    piece_ids = jnp.arange(piece.shape[1], dtype=jnp.int32)
    chosen = ((wanted[:, None] == piece_ids[None, :]) & valid[:, None]).astype(jnp.float32)
    extended = jnp.einsum("kn,pnfx->pkfx", chosen, piece, precision=lax.Precision.HIGHEST)
    seam_rows = jnp.concatenate([extended[..., :EDGE], extended[..., KEEP + EDGE :]], axis=-1)
    widened = with_halo(seam_rows, (("tm", 1),), 1)
    upper_rim = widened[:, 2:, :, :EDGE]
    lower_rim = widened[:, :CH_DEV, :, EDGE:]
    stitched = stitch_bands(extended, upper_rim, lower_rim, slot_ids, band_width, KEEP, EDGE)
    fine_count = stitched.shape[2]
    result = jnp.transpose(stitched, (0, 2, 1, 3)).reshape(2, fine_count, CH_DEV * KEEP)
    return result[None, None]


def solution(mesh):
    placed = (P("pol", "groups", ("tm", "zoom")), P(), P(), P("groups"), P("groups"))
    return jax.shard_map(
        on_device,
        mesh=mesh,
        in_specs=placed,
        out_specs=P("pol", "zoom", "groups", None, "tm"),
        check_vma=False,
    )
```

profile of v0, /device:TPU:0, one launch (start us, length us, event | category | flops | bytes accessed | tf_op | source)
XLA Modules:
  0.0 742.3 jit_solution(14112968930927286851)
XLA Ops:
  30.5 136.5 %fusion.2 = (bf16[2,933552]{1,0:T(2,128)(2,1)}, bf16[2,933552]{1,0:T(2,128)(2,1)}, bf16[2,933552]{1,0:T(2,128)(2,1)}, bf16[2,933552]{1,0:T(2,128)(2,1)}, bf16[2,...) fusion(bf16[2,5712]{1,0:T(2,128)(2,1)S(1)} %collective-permute-done, bf16[2,933120]{1,0:T(2,128)(2,1)} %bitcast.123), kind=kLoop, calls=%fused_computation.30 | loop fusion | flops 44810496 | bytes 26160576 | tf_op jit(solution)/shard_map/concatenate | solution.py:143
  176.2 13.3 %reshape.600 = bf16[2,2161,432]{2,1,0:T(8,128)(2,1)} reshape(bf16[1867104]{0:T(1024)(128)(2,1)} %reshape.688) | data formatting | bytes 7468416 | tf_op jit(solution)/shard_map/reshape | solution.py:71
  189.5 9.1 %reshape.686 = bf16[1867104]{0:T(1024)(128)(2,1)} reshape(bf16[2,933552]{1,0:T(2,128)(2,1)} %get-tuple-element.44) | data formatting | bytes 7468416
  198.6 13.1 %reshape.601 = bf16[2,2161,432]{2,1,0:T(8,128)(2,1)} reshape(bf16[1867104]{0:T(1024)(128)(2,1)} %reshape.686) | data formatting | bytes 7468416 | tf_op jit(solution)/shard_map/reshape | solution.py:71
  211.7 9.1 %reshape.684 = bf16[1867104]{0:T(1024)(128)(2,1)} reshape(bf16[2,933552]{1,0:T(2,128)(2,1)} %get-tuple-element.45) | data formatting | bytes 7468416
  220.9 13.1 %reshape.602 = bf16[2,2161,432]{2,1,0:T(8,128)(2,1)} reshape(bf16[1867104]{0:T(1024)(128)(2,1)} %reshape.684) | data formatting | bytes 7468416 | tf_op jit(solution)/shard_map/reshape | solution.py:71
  243.1 13.4 %reshape.603 = bf16[2,2161,432]{2,1,0:T(8,128)(2,1)} reshape(bf16[1867104]{0:T(1024)(128)(2,1)} %reshape.682) | data formatting | bytes 7468416 | tf_op jit(solution)/shard_map/reshape | solution.py:71
  256.5 9.3 %reshape.680 = bf16[1867104]{0:T(1024)(128)(2,1)} reshape(bf16[2,933552]{1,0:T(2,128)(2,1)} %get-tuple-element.47) | data formatting | bytes 7468416
  265.7 12.9 %reshape.604 = bf16[2,2161,432]{2,1,0:T(8,128)(2,1)} reshape(bf16[1867104]{0:T(1024)(128)(2,1)} %reshape.680) | data formatting | bytes 7468416 | tf_op jit(solution)/shard_map/reshape | solution.py:71
  278.7 9.6 %reshape.678 = bf16[1867104]{0:T(1024)(128)(2,1)} reshape(bf16[2,933552]{1,0:T(2,128)(2,1)} %get-tuple-element.48) | data formatting | bytes 7468416
  288.3 12.9 %reshape.605 = bf16[2,2161,432]{2,1,0:T(8,128)(2,1)} reshape(bf16[1867104]{0:T(1024)(128)(2,1)} %reshape.678) | data formatting | bytes 7468416 | tf_op jit(solution)/shard_map/reshape | solution.py:71
  301.2 106.8 %fusion.8 = (bf16[2,933552]{1,0:T(2,128)(2,1)}, bf16[2,933552]{1,0:T(2,128)(2,1)}, bf16[2,933552]{1,0:T(2,128)(2,1)}, bf16[2,933552]{1,0:T(2,128)(2,1)}, bf16[2,933552]{1,0:T(2,128)(2,1)}) fusion(bf16[2,5712]{1,0:T(2,128)(2,1)S(1)} %collective-permute-done, bf16[2,933120]{1,0:T(2,128)(2,1)} %bitcast.124), kind=kLoop, calls=%fused_computation.36 | loop fusion | flops 37342080 | bytes 22426368 | tf_op jit(solution)/shard_map/concatenate | solution.py:143
  417.1 13.2 %reshape.606 = bf16[2,2161,432]{2,1,0:T(8,128)(2,1)} reshape(bf16[1867104]{0:T(1024)(128)(2,1)} %reshape.676) | data formatting | bytes 7468416 | tf_op jit(solution)/shard_map/reshape | solution.py:71
  439.3 13.3 %reshape.607 = bf16[2,2161,432]{2,1,0:T(8,128)(2,1)} reshape(bf16[1867104]{0:T(1024)(128)(2,1)} %reshape.674) | data formatting | bytes 7468416 | tf_op jit(solution)/shard_map/reshape | solution.py:71
  461.7 13.1 %reshape.608 = bf16[2,2161,432]{2,1,0:T(8,128)(2,1)} reshape(bf16[1867104]{0:T(1024)(128)(2,1)} %reshape.672) | data formatting | bytes 7468416 | tf_op jit(solution)/shard_map/reshape | solution.py:71
  483.8 13.1 %reshape.609 = bf16[2,2161,432]{2,1,0:T(8,128)(2,1)} reshape(bf16[1867104]{0:T(1024)(128)(2,1)} %reshape.670) | data formatting | bytes 7468416 | tf_op jit(solution)/shard_map/reshape | solution.py:71
  496.9 9.4 %reshape.668 = bf16[1867104]{0:T(1024)(128)(2,1)} reshape(bf16[2,933552]{1,0:T(2,128)(2,1)} %get-tuple-element.52) | data formatting | bytes 7468416
  506.4 12.9 %reshape.610 = bf16[2,2161,432]{2,1,0:T(8,128)(2,1)} reshape(bf16[1867104]{0:T(1024)(128)(2,1)} %reshape.668) | data formatting | bytes 7468416 | tf_op jit(solution)/shard_map/reshape | solution.py:71
  538.9 13.1 %reshape.611 = bf16[2,2161,432]{2,1,0:T(8,128)(2,1)} reshape(bf16[1867104]{0:T(1024)(128)(2,1)} %reshape.666) | data formatting | bytes 7468416 | tf_op jit(solution)/shard_map/reshape | solution.py:71
  552.0 14.9 %fusion.79 = (bf16[2,2160,432]{2,1,0:T(8,128)(2,1)}, bf16[2,2160,432]{2,1,0:T(8,128)(2,1)}, bf16[2,2160,432]{2,1,0:T(8,128)(2,1)}, bf16[2,2160,432]{2,1,0:T(8,128)(2,1)}) fusion(bf16[2,2161,432]{2,1,0:T(8,128)(2,1)} %reshape.600, bf16[2,2161,432]{2,1,0:T(8,128)(2,1)} %reshape.601), kind=kLoop, calls=%fused_computation.177 | loop fusion | bytes 29859840 | tf_op jit(solution)/shard_map/slice | solution.py:75
  567.0 12.9 %fusion.81 = (bf16[2,2160,432]{2,1,0:T(8,128)(2,1)}, bf16[2,2160,432]{2,1,0:T(8,128)(2,1)}, bf16[2,2160,432]{2,1,0:T(8,128)(2,1)}, bf16[2,2160,432]{2,1,0:T(8,128)(2,1)}) fusion(bf16[2,2161,432]{2,1,0:T(8,128)(2,1)S(1)} %bitcast.105, bf16[2,2161,432]{2,1,0:T(8,128)(2,1)} %reshape.603), kind=kLoop, calls=%fused_computation.179 | loop fusion | bytes 29859840 | tf_op jit(solution)/shard_map/slice | solution.py:75
  611.2 32.1 %bitcast_convert_fusion = bf16[2,512,2160]{1,2,0:T(8,128)(2,1)} fusion(bf16[2,2160,432]{2,1,0:T(8,128)(2,1)} %get-tuple-element.100, bf16[2,2160,432]{2,1,0:T(8,128)(2,1)} %get-tuple-element.101, bf16[2,2160,432]{2,1,0:T(8,128)(2,1)} %get-tuple-element.40, bf16[2,2160,432]{2,1,0:T(8,128)(2,1)} %get-tuple-element.39, ...), kind=kOutput, calls=%fused_computation.3 | convolution fusion | flops 4692361216 | bytes 96124928 | tf_op jit(solution)/shard_map/pqkn,qsn->pks/dot_general | solution.py:147
  643.3 12.2 %copy.70 = bf16[2,512,2160]{2,0,1:T(2,128)(2,1)} copy(bf16[2,512,2160]{1,2,0:T(8,128)(2,1)} %bitcast_convert_fusion) | data formatting | bytes 8847360 | tf_op jit(solution)/shard_map/convert_element_type | solution.py:149
  700.4 31.8 %all_gather.3 = f32[2,24,1,3172]{3,0,2,1:T(2,128)S(1)} all-gather(f32[2,3,1,3172]{3,0,2,1:T(2,128)S(1)} %pad_maximum_fusion.13), channel_id=1, replica_groups=mesh['groups'=2,'tm'=4,'zoom'=2,'pol'=2] {'tm','zoom'}, dimensions={1}, use_global_device_ids=true | all-gather | bytes 685152 | tf_op jit(solution)/shard_map/all_gather | solution.py:175
  (170 shorter events, 189.9 us)
Async XLA Ops:
  0.8 20.4 %copy-start.10 = (f32[12,512]{1,0:T(8,128)S(1)}, f32[12,512]{1,0:T(8,128)}, u32[]{:S(2)}) copy-start(f32[12,512]{1,0:T(8,128)} %param.10) | copy-start | bytes 73732
  0.8 20.4 %copy-start.18 = (s32[2]{0:T(128)S(1)}, s32[2]{0:T(128)}, u32[]{:S(2)}) copy-start(s32[2]{0:T(128)} %param.13) | copy-start | bytes 28
  0.8 21.4 %copy-start.16 = (s32[2]{0:T(128)S(1)}, s32[2]{0:T(128)}, u32[]{:S(2)}) copy-start(s32[2]{0:T(128)} %param.12) | copy-start | bytes 28
  0.8 22.4 %copy-start.12 = (s32[3172]{0:T(1024)S(1)}, s32[3172]{0:T(1024)}, u32[]{:S(2)}) copy-start(s32[3172]{0:T(1024)} %constant.143) | copy-start | bytes 38068
  0.8 23.0 %copy-start.11 = (s32[3172]{0:T(1024)S(1)}, s32[3172]{0:T(1024)}, u32[]{:S(2)}) copy-start(s32[3172]{0:T(1024)} %constant.144) | copy-start | bytes 38068
  0.8 29.7 %collective-permute-start = (bf16[2,5712]{1,0:T(2,128)(2,1)S(1)}, bf16[2,5712]{1,0:T(2,128)(2,1)S(1)}, u32[]{:S(2)}, u32[]{:S(2)}) collective-permute-start(bf16[2,5712]{1,0:T(2,128)(2,1)S(1)} %slice.375), channel_id=1, source_target_pairs={{2,0},{4,2},{6,4},{8,6},{10,8},{12,10},{14,12},{3,1},{5,3},{7,5},{... | collective-permute-start | bytes 68552 | tf_op jit(solution)/shard_map/ppermute | solution.py:21
  538.9 28.0 %slice-start = ((s8[4440064]{0:T(1024)(128)(4,1)}), s8[245760]{0:T(1024)(128)(4,1)S(1)}, s32[]{:S(2)}) async-start(s8[4440064]{0:T(1024)(128)(4,1)} %bitcast.104), calls=%async_computation.1 | async-start | bytes 491520
  552.0 27.9 %slice-start.2 = ((s8[4440064]{0:T(1024)(128)(4,1)}), s8[4194304]{0:T(1024)(128)(4,1)S(1)}, s32[]{:S(2)}) async-start(s8[4440064]{0:T(1024)(128)(4,1)} %bitcast.106), calls=%async_computation.3 | async-start | bytes 8388608
  552.0 27.9 %slice-start.4 = ((s8[4440064]{0:T(1024)(128)(4,1)}), s8[4194304]{0:T(1024)(128)(4,1)S(1)}, s32[]{:S(2)}) async-start(s8[4440064]{0:T(1024)(128)(4,1)} %bitcast.108), calls=%async_computation.5 | async-start | bytes 8388608
  567.0 21.5 %slice-start.6 = ((s8[4440064]{0:T(1024)(128)(4,1)}), s8[4194304]{0:T(1024)(128)(4,1)S(1)}, s32[]{:S(2)}) async-start(s8[4440064]{0:T(1024)(128)(4,1)} %bitcast.110), calls=%async_computation.7 | async-start | bytes 8388608
  567.0 21.5 %slice-start.10 = ((s8[4440064]{0:T(1024)(128)(4,1)}), s8[4194304]{0:T(1024)(128)(4,1)S(1)}, s32[]{:S(2)}) async-start(s8[4440064]{0:T(1024)(128)(4,1)} %bitcast.114), calls=%async_computation.11 | async-start | bytes 8388608
  643.3 26.2 %copy-start.6 = (f32[5,3456]{1,0:T(8,128)S(1)}, f32[5,3456]{1,0:T(8,128)}, u32[]{:S(2)}) copy-start(f32[5,3456]{1,0:T(8,128)} %param.11) | copy-start | bytes 207364
  643.3 26.4 %copy-start.14 = (f32[5]{0:T(128)S(1)}, f32[5]{0:T(128)}, u32[]{:S(2)}) copy-start(f32[5]{0:T(128)} %get-tuple-element.108) | copy-start | bytes 64
  643.3 26.4 %copy-start.17 = (f32[128]{0:T(128)S(1)}, f32[128]{0:T(128)}, u32[]{:S(2)}) copy-start(f32[128]{0:T(128)} %add_multiply_fusion) | copy-start | bytes 1540
  643.3 34.0 %copy-start.1 = (bf16[1,2,27,27]{3,2,1,0:T(8,128)(2,1)S(1)}, bf16[1,2,27,27]{3,2,1,0:T(8,128)(2,1)}, u32[]{:S(2)}) copy-start(bf16[1,2,27,27]{3,2,1,0:T(8,128)(2,1)} %get-tuple-element.81) | copy-start | bytes 8752
  643.3 34.0 %copy-start.2 = (bf16[1,2,27,27]{3,2,1,0:T(8,128)(2,1)S(1)}, bf16[1,2,27,27]{3,2,1,0:T(8,128)(2,1)}, u32[]{:S(2)}) copy-start(bf16[1,2,27,27]{3,2,1,0:T(8,128)(2,1)} %get-tuple-element.82) | copy-start | bytes 8752
  655.6 22.0 %copy-start.3 = (f32[27,128]{1,0:T(8,128)S(1)}, f32[27,128]{1,0:T(8,128)}, u32[]{:S(2)}) copy-start(f32[27,128]{1,0:T(8,128)} %get-tuple-element.104) | copy-start | bytes 41476
  655.6 22.0 %copy-start.4 = (f32[27,128]{1,0:T(8,128)S(1)}, f32[27,128]{1,0:T(8,128)}, u32[]{:S(2)}) copy-start(f32[27,128]{1,0:T(8,128)} %get-tuple-element.105) | copy-start | bytes 41476
  655.6 22.0 %copy-start.7 = (bf16[128,128]{1,0:T(8,128)(2,1)S(1)}, bf16[128,128]{1,0:T(8,128)(2,1)}, u32[]{:S(2)}) copy-start(bf16[128,128]{1,0:T(8,128)(2,1)} %get-tuple-element.106) | copy-start | bytes 98308
  655.6 22.0 %copy-start.8 = (bf16[128,128]{1,0:T(8,128)(2,1)S(1)}, bf16[128,128]{1,0:T(8,128)(2,1)}, u32[]{:S(2)}) copy-start(bf16[128,128]{1,0:T(8,128)(2,1)} %get-tuple-element.107) | copy-start | bytes 98308
  655.6 22.0 %copy-start.9 = (bf16[128,128]{1,0:T(8,128)(2,1)S(1)}, bf16[128,128]{1,0:T(8,128)(2,1)}, u32[]{:S(2)}) copy-start(bf16[128,128]{1,0:T(8,128)(2,1)} %fusion.54) | copy-start | bytes 98308
  660.0 16.3 %all-to-all-start = ((bf16[2,3,8,2160]{3,0,1,2:T(2,128)(2,1)}), bf16[2,3,8,2160]{3,0,1,2:T(2,128)(2,1)S(1)}, u32[]{:S(2)}, u32[]{:S(2)}) async-start(bf16[2,3,8,2160]{3,0,1,2:T(2,128)(2,1)} %copy.72), calls=%async_computation | async-start | bytes 417792 | tf_op jit(solution)/shard_map/all_to_all | solution.py:170
  733.2 3.5 collective-permute-start.1
  734.5 5.5 collective-permute-start.2
  (17 other events, 193.4 us)
where the time goes:
time: 750 us; the launch traced here: 742 us
  local copies, waits for them, and re-layouts  387 us (52%)
  other arithmetic  266 us (35%)
  matrix products  34 us (5%)
  blocking collectives  31.8 us (4%)
  starting transfers between devices  12.4 us (2%)
  waiting for transfers between devices  9.08 us (1%)
    concatenate x2, other arithmetic, on_device(): jnp.concatenate([signal, following, jnp.zeros((2, pieces * HOP), jnp.bflo...  243 us
    reshape x12, local copies, waits for them, and re-layouts, frame_view(): segment[:, :(spectra + pieces - 1) * hop_len]  157 us
    unnamed x88, local copies, waits for them, and re-layouts  120 us
    slice x6, local copies, waits for them, and re-layouts, frame_view(): framed[:, offset:offset + spectra]  58.8 us
    dot_general x1, matrix products, on_device(): jnp.einsum('pqkn,qsn->pks', rotation_block(chan_len), weighted, preferred...  32.1 us
    all_gather x1, blocking collectives, on_device(): piece = lax.all_gather(computed, ('tm', 'zoom'), axis=1, tiled=True)  31.8 us
  transfers between devices with their start and end apart: 4, of which 2 were waited for; matrix products, arithmetic and copies ran while one was open for 4% of the time, Pallas kernels for 0%

commit v1 on v0

--- a/solution.py
+++ b/solution.py
@@ -1,9 +1,12 @@
+import functools
 import math
 
 import jax
 import jax.numpy as jnp
 import numpy as np
 from jax import lax
+from jax.experimental import pallas as pl
+from jax.experimental.pallas import tpu as pltpu
 from jax.sharding import PartitionSpec as P
 
 HOP = 432
@@ -133,7 +136,7 @@
     return joined * live
 
 
-def on_device(voltages, section1_taps, section2_taps, band_starts, band_widths):
+def general_plan(voltages, section1_taps, section2_taps, band_starts, band_widths):
     signal = voltages[0]
     tap_count, chan_len = section1_taps.shape
     spectra = signal.shape[1] // HOP
@@ -186,8 +189,305 @@
     return result[None, None]
 
 
+ROWS = 8
+LANES = 128
+SLOT_LANES = 2 * ROWS
+NT = (((1,), (1,)), ((), ()))
+
+
+def sine_quarter(value):
+    square = value * value
+    total = -3.5988432e-06
+    for factor in (1.604411848e-04, -4.6817541353e-03, 7.96926262462e-02, -6.459640975062e-01):
+        total = total * square + factor
+    return (total * square + 1.5707963267949) * value
+
+
+def section_one_kernel(plan, starts_ref, widths_ref, taps_ref, signal_ref, *rest):
+    (outs, (table, taps_rows, frames, total, sems)) = (rest[: plan.devices], rest[plan.devices :])
+    blocks, chan_len, live = (plan.blocks, plan.chan_len, plan.live)
+    half = ROWS * live
+    columns = 2 * half
+    lead = plan.lead
+    copies = [
+        pltpu.make_async_copy(
+            signal_ref.at[:, block], frames.at[block, pl.ds(lead, plan.local_rows)], sems.at[block]
+        )
+        for block in range(blocks)
+    ]
+    for copy in copies:
+        copy.start()
+    edge = jnp.zeros((blocks, lead, 2, LANES), jnp.bfloat16)
+    frames[:, :lead] = edge
+    frames[:, lead + plan.local_rows :] = edge
+
+    row = lax.broadcasted_iota(jnp.int32, (columns, 1), 0)
+    imag = (row >= half).astype(jnp.int32)
+    shift = (row - imag * half) // live
+    ident = row - imag * half - shift * live
+    channel = jnp.zeros((columns, 1), jnp.int32)
+    first = jnp.int32(0)
+    firsts = []
+    for band in range(plan.bands):
+        inside = (ident >= first) & (ident < first + widths_ref[band])
+        channel = jnp.where(inside, starts_ref[band] + ident - first, channel)
+        firsts.append(first)
+        first = first + widths_ref[band]
+    phase = lax.broadcasted_iota(jnp.int32, (columns, chan_len), 1) - HOP * shift
+    turn = (channel * phase + imag * (chan_len // 4)) & (chan_len - 1)
+    quarter = chan_len // 4
+    folded = jnp.abs(turn - 2 * quarter)
+    angle = (folded - quarter).astype(jnp.float32) * (1.0 / quarter)
+    rotation = sine_quarter(angle).astype(jnp.bfloat16).astype(jnp.float32)
+
+    flat = jnp.concatenate(
+        [jnp.broadcast_to(taps_ref[tap : tap + 1, :], (8, chan_len)) for tap in range(plan.taps)]
+        + [jnp.zeros((8, plan.depth - plan.taps * chan_len), jnp.float32)],
+        axis=1,
+    )
+    for shift_index in range(ROWS):
+        taps_rows[shift_index] = (
+            pltpu.roll(flat, HOP * shift_index, axis=1) if shift_index else flat
+        )
+    for piece in range(plan.depth // chan_len):
+        span = pl.ds(piece * chan_len, chan_len)
+        scale = jnp.concatenate(
+            [
+                jnp.broadcast_to(
+                    taps_rows[shift_index, :, span][None], (live // 8, 8, chan_len)
+                ).reshape(live, chan_len)
+                for shift_index in range(ROWS)
+            ],
+            axis=0,
+        )
+        for part in range(2):
+            table[pl.ds(part * half, half), span] = (
+                scale * rotation[part * half : (part + 1) * half]
+            ).astype(jnp.bfloat16)
+
+    for copy in copies:
+        copy.wait()
+    count = 2 * plan.out_rows
+    pairs = frames.reshape(blocks, 2 * (plan.local_rows + 2 * lead), LANES)
+    acc = jnp.zeros((count, columns), jnp.float32)
+    for index in range(0, plan.depth // LANES, 2):
+        left = jnp.concatenate(
+            [
+                pairs[(index + step) % blocks, pl.ds(2 * ((index + step) // blocks), count), :]
+                for step in range(2)
+            ],
+            axis=1,
+        )
+        right = table[:, index * LANES : (index + 2) * LANES]
+        acc = acc + lax.dot_general(left, right, NT, preferred_element_type=jnp.float32)
+    for tile in range(columns // LANES):
+        total[tile] = acc[:, tile * LANES : (tile + 1) * LANES]
+    (real_rows, imag_rows) = (
+        jnp.concatenate(
+            [total[tile, pl.ds(part, plan.out_rows, 2), :] for tile in range(columns // LANES)],
+            axis=1,
+        )
+        for part in range(2)
+    )
+    lane = lax.broadcasted_iota(jnp.int32, (1, columns), 1)
+    sign = jnp.where(lane < half, -1.0, 1.0)
+    coarse = (real_rows + sign * pltpu.roll(imag_rows, half, axis=1)).astype(jnp.bfloat16)
+
+    here = lax.axis_index("tm") * plan.zooms + lax.axis_index("zoom")
+    code = ident * SLOT_LANES + imag * ROWS + shift
+    out_lane = lax.broadcasted_iota(jnp.int32, (1, LANES), 1)
+    slot = out_lane // SLOT_LANES
+    for step in range(plan.devices):
+        target = jnp.bitwise_xor(here, step)
+        (target_tm, target_zoom) = (target // plan.zooms, target % plan.zooms)
+        (band_first, width) = (jnp.int32(0), jnp.int32(0))
+        for band in range(plan.bands):
+            band_first = jnp.where(target_zoom == band, firsts[band], band_first)
+            width = jnp.where(target_zoom == band, widths_ref[band], width)
+        base = target_tm * CH_DEV - 1
+        position = base + slot
+        valid = (position >= 0) & (position < width) & (slot < CH_DEV + 2)
+        wanted = jnp.where(valid, (band_first + base) * SLOT_LANES + out_lane, -1)
+        pick = (code == wanted).astype(jnp.float32).astype(jnp.bfloat16)
+        outs[step][...] = lax.dot_general(
+            coarse, pick, (((1,), (0,)), ((), ())), preferred_element_type=jnp.float32
+        ).astype(jnp.bfloat16)
+
+
+def section_two_kernel(plan, widths_ref, taps_ref, dft_ref, cos_ref, sin_ref, join_ref, *rest):
+    (blocks, out_ref, series) = (rest[: plan.devices], rest[plan.devices], rest[plan.devices + 1])
+    here = lax.axis_index("tm") * plan.zooms + lax.axis_index("zoom")
+    fine_rows = plan.fine_rows
+    pad = 8
+    series[...] = jnp.zeros_like(series)
+    for step in range(plan.devices):
+        source = jnp.bitwise_xor(here, step)
+        span = pl.ds(source * plan.local_rows + (pad - plan.lead), plan.out_rows)
+        series[span, :] += blocks[step][...].astype(jnp.float32)
+    fine_in = jnp.zeros((fine_rows, LANES), jnp.float32)
+    for tap in range(plan.fine_taps):
+        fine_in = fine_in + taps_ref[tap] * series[pl.ds(pad + tap * fine_rows, fine_rows), :]
+    spun = lax.dot_general(
+        dft_ref[...],
+        fine_in.astype(jnp.bfloat16),
+        (((1,), (0,)), ((), ())),
+        preferred_element_type=jnp.float32,
+    )
+    (even, odd) = (spun[:fine_rows], spun[fine_rows:])
+    (cosine_tab, sine_tab) = (cos_ref[...], sin_ref[...])
+    mixed = jnp.concatenate(
+        [
+            (part * factor).astype(jnp.bfloat16)
+            for part in (even, odd)
+            for factor in (cosine_tab, sine_tab)
+        ],
+        axis=1,
+    )
+    out_ref[...] = lax.dot_general(
+        join_ref[...], mixed, NT, preferred_element_type=jnp.float32
+    )
+
+
+def fine_tables(fine_rows):
+    fine_len = fine_rows * ROWS
+    offset = KEEP // 2 + EDGE
+    bins = np.arange(fine_rows) - offset
+    spin = 2.0 * np.pi * (np.outer(bins, np.arange(fine_rows)) % fine_rows) / fine_rows
+    dft = np.concatenate([np.cos(spin), np.sin(spin)], axis=0)
+    twist = 2.0 * np.pi * (np.outer(bins, np.arange(LANES) % ROWS) % fine_len) / fine_len
+    join = np.zeros((ROWS, 2, LANES // SLOT_LANES, 4, LANES // SLOT_LANES, 2, ROWS))
+    turn = 2.0 * np.pi * (np.outer(np.arange(ROWS), np.arange(ROWS)) % ROWS) / ROWS
+    (cosine, sine) = (np.cos(turn), np.sin(turn))
+    for slot in range(LANES // SLOT_LANES):
+        real, imag = (join[:, 0, slot, :, slot], join[:, 1, slot, :, slot])
+        real[:, 0, 0], real[:, 0, 1] = (cosine, sine)
+        real[:, 1, 0], real[:, 1, 1] = (-sine, cosine)
+        real[:, 2, 0], real[:, 2, 1] = (-sine, cosine)
+        real[:, 3, 0], real[:, 3, 1] = (-cosine, -sine)
+        imag[:, 0, 0], imag[:, 0, 1] = (-sine, cosine)
+        imag[:, 1, 0], imag[:, 1, 1] = (-cosine, -sine)
+        imag[:, 2, 0], imag[:, 2, 1] = (-cosine, -sine)
+        imag[:, 3, 0], imag[:, 3, 1] = (sine, -cosine)
+    return (
+        jnp.asarray(dft, jnp.bfloat16),
+        jnp.asarray(np.cos(twist), jnp.float32),
+        jnp.asarray(np.sin(twist), jnp.float32),
+        jnp.asarray(join.reshape(LANES, 4 * LANES), jnp.bfloat16),
+    )
+
+
+class Plan:
+    def __init__(self, mesh, samples, bands, section1_shape, section2_shape):
+        (self.tms, self.zooms) = (mesh.shape["tm"], mesh.shape["zoom"])
+        self.devices = self.tms * self.zooms
+        self.bands = bands
+        (self.taps, self.chan_len) = section1_shape
+        self.fine_taps = section2_shape[0]
+        self.live = LIVE_DEV * self.devices
+        self.samples = samples
+        self.row_len = ROWS * HOP
+        self.blocks = self.row_len // LANES
+        self.local_rows = samples // self.row_len
+        reach = (ROWS - 1) * HOP + self.taps * self.chan_len
+        unit = max(self.chan_len, 2 * LANES)
+        self.depth = -(-reach // unit) * unit
+        self.lead = -(-self.depth // self.row_len) - 1
+        self.out_rows = self.local_rows + self.lead
+        self.fine_rows = section2_shape[1] // ROWS
+
+    def fits(self, section2_shape):
+        return (
+            self.row_len % LANES == 0
+            and self.samples % self.row_len == 0
+            and self.chan_len & (self.chan_len - 1) == 0
+            and self.chan_len % LANES == 0
+            and self.devices & (self.devices - 1) == 0
+            and self.live % 8 == 0
+            and (2 * ROWS * self.live) % LANES == 0
+            and 2 * ROWS * self.live <= 4 * LANES
+            and (CH_DEV + 2) * SLOT_LANES <= LANES
+            and self.out_rows % 16 == 0
+            and self.fine_rows % 16 == 0
+            and section2_shape[1] % ROWS == 0
+            and self.devices * self.samples == HOP * self.fine_taps * section2_shape[1]
+        )
+
+
+def direct_plan(plan, voltages, section1_taps, section2_taps, band_starts, band_widths):
+    signal = voltages[0].reshape(2, plan.local_rows, plan.blocks, LANES).transpose(1, 2, 0, 3)
+    smem = pl.BlockSpec(memory_space=pltpu.SMEM)
+    vmem = pl.BlockSpec(memory_space=pltpu.VMEM)
+    columns = 2 * ROWS * plan.live
+    block = jax.ShapeDtypeStruct((plan.out_rows, LANES), jnp.bfloat16)
+    sent = pl.pallas_call(
+        functools.partial(section_one_kernel, plan),
+        out_shape=[block] * plan.devices,
+        in_specs=[smem, smem, vmem, pl.BlockSpec(memory_space=pl.ANY)],
+        out_specs=[vmem] * plan.devices,
+        scratch_shapes=[
+            pltpu.VMEM((columns, plan.depth), jnp.bfloat16),
+            pltpu.VMEM((ROWS, 8, plan.depth), jnp.float32),
+            pltpu.VMEM((plan.blocks, plan.local_rows + 2 * plan.lead, 2, LANES), jnp.bfloat16),
+            pltpu.VMEM((columns // LANES, 2 * plan.out_rows, LANES), jnp.float32),
+            pltpu.SemaphoreType.DMA((plan.blocks,)),
+        ],
+        compiler_params=pltpu.CompilerParams(vmem_limit_bytes=40 * 2**20),
+        name="section_one",
+    )(band_starts, band_widths, section1_taps, signal)
+    received = [sent[0]]
+    for step in range(1, plan.devices):
+        pairs = [(index, index ^ step) for index in range(plan.devices)]
+        received.append(lax.ppermute(sent[step], ("tm", "zoom"), pairs))
+    fine_rows = plan.fine_rows
+    spread = jnp.tile(
+        section2_taps.reshape(plan.fine_taps, fine_rows, ROWS), (1, 1, LANES // ROWS)
+    )
+    (dft, cosine_tab, sine_tab, join) = fine_tables(fine_rows)
+    bins = pl.pallas_call(
+        functools.partial(section_two_kernel, plan),
+        out_shape=jax.ShapeDtypeStruct((LANES, fine_rows), jnp.float32),
+        in_specs=[smem] + [vmem] * (5 + plan.devices),
+        out_specs=vmem,
+        scratch_shapes=[
+            pltpu.VMEM((plan.fine_taps * fine_rows + 16 + plan.lead, LANES), jnp.float32)
+        ],
+        compiler_params=pltpu.CompilerParams(vmem_limit_bytes=24 * 2**20),
+        name="section_two",
+    )(band_widths, spread, dft, cosine_tab, sine_tab, join, *received)
+    slots = LANES // SLOT_LANES
+    whole = bins.reshape(ROWS, 2, slots, fine_rows).transpose(1, 2, 0, 3)
+    whole = whole.reshape(2, slots, 1, ROWS * fine_rows)
+    zoom = lax.axis_index("zoom")
+    band_width = jnp.sum(jnp.where(jnp.arange(plan.bands) == zoom, band_widths, 0))
+    slot_ids = lax.axis_index("tm") * CH_DEV + jnp.arange(CH_DEV, dtype=jnp.int32)
+    stitched = stitch_bands(
+        whole[:, 1 : CH_DEV + 1],
+        whole[:, 2 : CH_DEV + 2, :, :EDGE],
+        whole[:, :CH_DEV, :, KEEP + EDGE : KEEP + 2 * EDGE],
+        slot_ids,
+        band_width,
+        KEEP,
+        EDGE,
+    )
+    return stitched.reshape(1, 1, 2, 1, CH_DEV * KEEP)
+
+
 def solution(mesh):
     placed = (P("pol", "groups", ("tm", "zoom")), P(), P(), P("groups"), P("groups"))
+
+    def on_device(voltages, section1_taps, section2_taps, band_starts, band_widths):
+        plan = Plan(
+            mesh,
+            voltages.shape[2],
+            band_widths.shape[0],
+            section1_taps.shape,
+            section2_taps.shape,
+        )
+        arrays = (voltages, section1_taps, section2_taps, band_starts, band_widths)
+        if plan.fits(section2_taps.shape):
+            return direct_plan(plan, *arrays)
+        return general_plan(*arrays)
+
     return jax.shard_map(
         on_device,
         mesh=mesh,

time: 750 us -> 44.5 us (0.06)
  local copies, waits for them, and re-layouts: 387 us -> 11.4 us
  other arithmetic: 266 us -> 2.23 us
  matrix products: 34 us -> 0 us
  blocking collectives: 31.8 us -> 0 us
  Pallas kernels: 0 us -> 12.6 us
    concatenate x3 -> x0, other arithmetic: 243 us -> none  [the longest x2 243 us: on_device(): jnp.concatenate([signal, following, jnp.zeros((2, pieces * HOP), jnp.bflo...]
    reshape x14 -> x2, local copies, waits for them, and re-layouts: 159 us -> 0.34 us  [the longest x1 0.18 us: direct_plan(): whole = whole.reshape(2, slots, 1, ROWS * fine_rows)]
    unnamed x88 -> x20, local copies, waits for them, and re-layouts: 120 us -> 4.15 us
    slice x12 -> x0, local copies, waits for them, and re-layouts: 67.7 us -> none  [the longest x6 58.8 us: frame_view(): framed[:, offset:offset + spectra]]
    dot_general x4 -> x0, matrix products: 34 us -> none  [the longest x1 32.1 us: on_device(): jnp.einsum('pqkn,qsn->pks', rotation_block(chan_len), weighted, preferred...]
    all_gather x1 -> x0, blocking collectives: 31.8 us -> none  [on_device(): piece = lax.all_gather(computed, ('tm', 'zoom'), axis=1, tiled=True)]
    gather x3 -> x0, local copies, waits for them, and re-layouts: 18.1 us -> none  [the longest x1 7.7 us: fine_spectra(): jnp.take(flattened, real_index, axis=2)]
    pallas_call x0 -> x2, Pallas kernels: none -> 12.6 us  [the longest x1 11 us: direct_plan(): pl.pallas_call(functools.partial(section_one_kernel, plan), out_shape=[bl...]
  transfers between devices with their start and end apart: 4 -> 7, of which waited for: 2 -> 2; matrix products, arithmetic and copies ran while one was open for 4% -> 18% of each run, Pallas kernels for 0% -> 0%
where the time goes in v1:
time: 44.5 us; the launch traced here: 44.2 us
  Pallas kernels  12.6 us (28%)
  starting transfers between devices  12.6 us (28%)
  local copies, waits for them, and re-layouts  11.4 us (26%)
  waiting for transfers between devices  5.2 us (12%)
  other arithmetic  2.23 us (5%)
    ppermute x7, starting transfers between devices, direct_plan(): received.append(lax.ppermute(sent[step], ('tm', 'zoom'), pairs))  12.6 us
    pallas_call x1, Pallas kernels, direct_plan(): pl.pallas_call(functools.partial(section_one_kernel, plan), out_shape=[bl...  11 us
    ppermute x7, waiting for transfers between devices, direct_plan(): received.append(lax.ppermute(sent[step], ('tm', 'zoom'), pairs))  5.2 us
    unnamed x20, local copies, waits for them, and re-layouts  4.15 us
    another operation x4, local copies, waits for them, and re-layouts, direct_plan(): jnp.tile(section2_taps.reshape(plan.fine_taps, fine_rows, ROWS), (1, 1, L...  4.04 us
    mul x3, local copies, waits for them, and re-layouts, stitch_bands(): return joined * live  2.5 us
    pallas_call x1, Pallas kernels, direct_plan(): pl.pallas_call(functools.partial(section_two_kernel, plan), out_shape=jax...  1.56 us
  transfers between devices with their start and end apart: 7, of which 2 were waited for; matrix products, arithmetic and copies ran while one was open for 18% of the time, Pallas kernels for 0%

profile of v1, /device:TPU:0, one launch (start us, length us, event | category | flops | bytes accessed | tf_op | source)
XLA Modules:
  0.0 44.2 jit_solution(12553594292020608721)
XLA Ops:
  0.0 2.1 %copy-done = bf16[1,2,933120]{2,1,0:T(2,128)(2,1)S(1)} copy-done((bf16[1,2,933120]{2,1,0:T(2,128)(2,1)S(1)}, bf16[1,2,933120]{2,1,0:T(2,128)(2,1)}, u32[]{:S(2)}) %copy-start) | copy-done | bytes 3732504
  2.1 0.8 %copy-done.5 = f32[12,512]{1,0:T(8,128)S(1)} copy-done((f32[12,512]{1,0:T(8,128)S(1)}, f32[12,512]{1,0:T(8,128)}, u32[]{:S(2)}) %copy-start.5) | copy-done | bytes 24600
  2.8 0.7 %copy-done.6 = s32[2]{0:T(128)S(1)} copy-done((s32[2]{0:T(128)S(1)}, s32[2]{0:T(128)}, u32[]{:S(2)}) %copy-start.6) | copy-done | bytes 32
  3.5 0.7 %copy-done.8 = s32[2]{0:T(128)S(1)} copy-done((s32[2]{0:T(128)S(1)}, s32[2]{0:T(128)}, u32[]{:S(2)}) %copy-start.8) | copy-done | bytes 32
  4.1 11.0 %section_one.1 = (bf16[272,128]{1,0:T(8,128)(2,1)S(1)}, bf16[272,128]{1,0:T(8,128)(2,1)S(1)}, bf16[272,128]{1,0:T(8,128)(2,1)S(1)}, bf16[272,128]{1,0:T(8,128)(2...) custom-call(s32[2]{0:T(128)S(1)} %copy-done.8, ...), custom_call_target="tpu_custom_call" | custom-call | tf_op jit(solution)/shard_map/section_one/pallas_call | solution.py:422
  15.2 3.0 %collective-permute-start = (bf16[272,128]{1,0:T(8,128)(2,1)S(1)}, bf16[272,128]{1,0:T(8,128)(2,1)S(1)}, u32[]{:S(2)}, u32[]{:S(2)}) collective-permute-start(bf16[272,128]{1,0:T(8,128)(2,1)S(1)} %get-tuple-element.14), channel_id=1, source_target_pairs={{0,2},{2,0},{4,6},{6,4},{8,10},{10,8},{12,14},{14,12},{1,3},{3,1},... | collective-permute-start | bytes 208904 | tf_op jit(solution)/shard_map/ppermute | solution.py:440
  18.2 1.6 %collective-permute-start.1 = (bf16[272,128]{1,0:T(8,128)(2,1)S(1)}, bf16[272,128]{1,0:T(8,128)(2,1)S(1)}, u32[]{:S(2)}, u32[]{:S(2)}) collective-permute-start(bf16[272,128]{1,0:T(8,128)(2,1)S(1)} %get-tuple-element.15), channel_id=1, source_target_pairs={{0,4},{2,6},{4,0},{6,2},{8,12},{10,14},{12,8},{14,10},{1,5},{3,7},... | collective-permute-start | bytes 208904 | tf_op jit(solution)/shard_map/ppermute | solution.py:440
  19.8 3.0 %collective-permute-start.3 = (bf16[272,128]{1,0:T(8,128)(2,1)S(1)}, bf16[272,128]{1,0:T(8,128)(2,1)S(1)}, u32[]{:S(2)}, u32[]{:S(2)}) collective-permute-start(bf16[272,128]{1,0:T(8,128)(2,1)S(1)} %get-tuple-element.17), channel_id=1, source_target_pairs={{0,8},{2,10},{4,12},{6,14},{8,0},{10,2},{12,4},{14,6},{1,9},{3,11}... | collective-permute-start | bytes 208904 | tf_op jit(solution)/shard_map/ppermute | solution.py:440
  22.8 1.3 %collective-permute-start.4 = (bf16[272,128]{1,0:T(8,128)(2,1)S(1)}, bf16[272,128]{1,0:T(8,128)(2,1)S(1)}, u32[]{:S(2)}, u32[]{:S(2)}) collective-permute-start(bf16[272,128]{1,0:T(8,128)(2,1)S(1)} %get-tuple-element.18), channel_id=1, source_target_pairs={{0,10},{2,8},{4,14},{6,12},{8,2},{10,0},{12,6},{14,4},{1,11},{3,9}... | collective-permute-start | bytes 208904 | tf_op jit(solution)/shard_map/ppermute | solution.py:440
  24.0 0.6 %tile.10 = f32[5,432,8]{2,1,0:T(8,128)S(1)} reshape(f32[5,3456]{1,0:T(8,128)S(1)} %copy-done.9) | data formatting | bytes 138240 | tf_op jit(solution)/shard_map/tile | solution.py:442
  24.7 0.4 copy.10
  25.0 1.2 %broadcast_bitcast_fusion = f32[5,432,128]{1,2,0:T(8,128)} fusion(f32[5,432,8]{1,2,0:T(8,128)S(1)} %copy.10), kind=kLoop, calls=%fused_computation | loop fusion | bytes 1175040 | tf_op jit(solution)/shard_map/tile | solution.py:442
  26.3 1.8 %copy.11.taps_ref = f32[5,432,128]{2,1,0:T(8,128)S(1)} copy(f32[5,432,128]{1,2,0:T(8,128)} %broadcast_bitcast_fusion) | data formatting | bytes 2211840 | tf_op jit(solution)/shard_map/tile | solution.py:442
  28.1 0.6 %fusion.2 = s32[]{:T(128)} fusion(s32[2]{0:T(128)S(1)} %copy-done.7, s32[]{:T(128)S(6)} %axis_index.28), kind=kLoop, calls=%fused_computation.18 | loop fusion | flops 5 | bytes 16 | tf_op jit(solution)/shard_map/reduce_sum | solution.py:461
  28.9 0.6 %compare_convert_fusion = (f32[5]{0:T(128)S(1)}, f32[5]{0:T(128)S(1)}) fusion(s32[]{:T(128)} %fusion.2, s32[]{:T(128)S(6)} %mul.99), kind=kLoop, calls=%fused_computation.14 | loop fusion | flops 40 | bytes 48 | tf_op jit(solution)/shard_map/convert_element_type | solution.py:126
  29.7 0.6 %compare_convert_fusion.1 = f32[5]{0:T(128)S(1)} fusion(s32[]{:T(128)} %fusion.2, s32[]{:T(128)S(6)} %mul.99), kind=kLoop, calls=%fused_computation.17 | loop fusion | flops 15 | bytes 28 | tf_op jit(solution)/shard_map/convert_element_type | solution.py:125
  30.3 3.7 %collective-permute-start.5 = (bf16[272,128]{1,0:T(8,128)(2,1)S(1)}, bf16[272,128]{1,0:T(8,128)(2,1)S(1)}, u32[]{:S(2)}, u32[]{:S(2)}) collective-permute-start(bf16[272,128]{1,0:T(8,128)(2,1)S(1)} %get-tuple-element.19), channel_id=1, source_target_pairs={{0,12},{2,14},{4,8},{6,10},{8,4},{10,6},{12,0},{14,2},{1,13},{3,15... | collective-permute-start | bytes 208904 | tf_op jit(solution)/shard_map/ppermute | solution.py:440
  34.1 0.8 %broadcast_reduce_fusion = f32[5,2916]{1,0:T(8,128)} fusion(f32[5]{0:T(128)S(1)} %compare_convert_fusion.1), kind=kLoop, calls=%fused_computation.3 | loop fusion | bytes 58340 | tf_op jit(solution)/shard_map/mul | solution.py:136
  34.8 1.0 %mul.114 = f32[14580]{0:T(1024)S(1)} reshape(f32[5,2916]{1,0:T(8,128)} %broadcast_reduce_fusion) | data formatting | bytes 116640 | tf_op jit(solution)/shard_map/mul | solution.py:136
  35.8 0.7 %collective-permute-done.5.rest_6_ = bf16[272,128]{1,0:T(8,128)(2,1)S(1)} collective-permute-done((bf16[272,128]{1,0:T(8,128)(2,1)S(1)}, bf16[272,128]{1,0:T(8,128)(2,1)S(1)}, u32[]{:S(2)}, u32[]{:S(2)}) %collective-permute-start.5) | collective-permute-done | bytes 69664 | tf_op jit(solution)/shard_map/ppermute | solution.py:440
  36.5 4.5 %collective-permute-done.6.rest_7_ = bf16[272,128]{1,0:T(8,128)(2,1)S(1)} collective-permute-done((bf16[272,128]{1,0:T(8,128)(2,1)S(1)}, bf16[272,128]{1,0:T(8,128)(2,1)S(1)}, u32[]{:S(2)}, u32[]{:S(2)}) %collective-permute-start.6) | collective-permute-done | bytes 69664 | tf_op jit(solution)/shard_map/ppermute | solution.py:440
  41.0 1.6 %section_two.1 = f32[128,432]{1,0:T(8,128)S(1)} custom-call(s32[2]{0:T(128)S(1)} %copy-done.7, f32[5,432,128]{2,1,0:T(8,128)S(1)} %copy.11.taps_ref, bf16[864,432]{1,0:T(8,128)(2,1)S(1)} %copy-done.1, f32[432,128]{1,0:T(8,128)S(1)} %copy-done.2, f32[432,128]{1,0:T(8,128)S(1)} %copy-done.3, bf16[128,512]{1,0:T(8,128)(2,1)S(1)} %copy-done.4, ...), custom_call_target="tpu_custom_call" | custom-call | tf_op jit(solution)/shard_map/section_two/pallas_call | solution.py:446
  43.1 0.2 concatenate.8
  43.4 0.8 %copy.13 = f32[1,1,2,1,14580]{4,3,2,1,0:T(1,128)} copy(f32[1,1,2,1,14580]{4,2,3,1,0:T(2,128)S(1)} %broadcast_multiply_fusion) | data formatting | bytes 233280 | tf_op jit(solution)/shard_map/mul | solution.py:136
  (35 shorter events, 0.9 us)
Async XLA Ops:
  0.0 2.1 %copy-start = (bf16[1,2,933120]{2,1,0:T(2,128)(2,1)S(1)}, bf16[1,2,933120]{2,1,0:T(2,128)(2,1)}, u32[]{:S(2)}) copy-start(bf16[1,2,933120]{2,1,0:T(2,128)(2,1)} %param.9) | copy-start | bytes 11197444
  2.1 0.8 %copy-start.5 = (f32[12,512]{1,0:T(8,128)S(1)}, f32[12,512]{1,0:T(8,128)}, u32[]{:S(2)}) copy-start(f32[12,512]{1,0:T(8,128)} %taps_ref.1) | copy-start | bytes 73732
  2.8 0.7 %copy-start.6 = (s32[2]{0:T(128)S(1)}, s32[2]{0:T(128)}, u32[]{:S(2)}) copy-start(s32[2]{0:T(128)} %widths_ref.3) | copy-start | bytes 28
  3.5 0.7 %copy-start.8 = (s32[2]{0:T(128)S(1)}, s32[2]{0:T(128)}, u32[]{:S(2)}) copy-start(s32[2]{0:T(128)} %starts_ref.1) | copy-start | bytes 28
  4.1 19.9 %copy-start.9 = (f32[5,3456]{1,0:T(8,128)S(1)}, f32[5,3456]{1,0:T(8,128)}, u32[]{:S(2)}) copy-start(f32[5,3456]{1,0:T(8,128)} %param.11) | copy-start | bytes 207364
  15.2 15.2 %collective-permute-start = (bf16[272,128]{1,0:T(8,128)(2,1)S(1)}, bf16[272,128]{1,0:T(8,128)(2,1)S(1)}, u32[]{:S(2)}, u32[]{:S(2)}) collective-permute-start(bf16[272,128]{1,0:T(8,128)(2,1)S(1)} %get-tuple-element.14), channel_id=1, source_target_pairs={{0,2},{2,0},{4,6},{6,4},{8,10},{10,8},{12,14},{14,12},{1,3},{3,1},... | collective-permute-start | bytes 208904 | tf_op jit(solution)/shard_map/ppermute | solution.py:440
  18.2 15.8 %collective-permute-start.1 = (bf16[272,128]{1,0:T(8,128)(2,1)S(1)}, bf16[272,128]{1,0:T(8,128)(2,1)S(1)}, u32[]{:S(2)}, u32[]{:S(2)}) collective-permute-start(bf16[272,128]{1,0:T(8,128)(2,1)S(1)} %get-tuple-element.15), channel_id=1, source_target_pairs={{0,4},{2,6},{4,0},{6,2},{8,12},{10,14},{12,8},{14,10},{1,5},{3,7},... | collective-permute-start | bytes 208904 | tf_op jit(solution)/shard_map/ppermute | solution.py:440
  19.7 16.1 %collective-permute-start.2 = (bf16[272,128]{1,0:T(8,128)(2,1)S(1)}, bf16[272,128]{1,0:T(8,128)(2,1)S(1)}, u32[]{:S(2)}, u32[]{:S(2)}) collective-permute-start(bf16[272,128]{1,0:T(8,128)(2,1)S(1)} %get-tuple-element.16), channel_id=1, source_target_pairs={{0,6},{2,4},{4,2},{6,0},{8,14},{10,12},{12,10},{14,8},{1,7},{3,5},... | collective-permute-start | bytes 208904 | tf_op jit(solution)/shard_map/ppermute | solution.py:440
  19.8 16.1 %collective-permute-start.3 = (bf16[272,128]{1,0:T(8,128)(2,1)S(1)}, bf16[272,128]{1,0:T(8,128)(2,1)S(1)}, u32[]{:S(2)}, u32[]{:S(2)}) collective-permute-start(bf16[272,128]{1,0:T(8,128)(2,1)S(1)} %get-tuple-element.17), channel_id=1, source_target_pairs={{0,8},{2,10},{4,12},{6,14},{8,0},{10,2},{12,4},{14,6},{1,9},{3,11}... | collective-permute-start | bytes 208904 | tf_op jit(solution)/shard_map/ppermute | solution.py:440
  22.8 13.1 %collective-permute-start.4 = (bf16[272,128]{1,0:T(8,128)(2,1)S(1)}, bf16[272,128]{1,0:T(8,128)(2,1)S(1)}, u32[]{:S(2)}, u32[]{:S(2)}) collective-permute-start(bf16[272,128]{1,0:T(8,128)(2,1)S(1)} %get-tuple-element.18), channel_id=1, source_target_pairs={{0,10},{2,8},{4,14},{6,12},{8,2},{10,0},{12,6},{14,4},{1,11},{3,9}... | collective-permute-start | bytes 208904 | tf_op jit(solution)/shard_map/ppermute | solution.py:440
  26.3 1.9 %copy-start.7 = (s32[2]{0:T(128)S(1)}, s32[2]{0:T(128)}, u32[]{:S(2)}) copy-start(s32[2]{0:T(128)} %widths_ref.3) | copy-start | bytes 28
  26.3 14.8 %copy-start.1 = (bf16[864,432]{1,0:T(8,128)(2,1)S(1)}, bf16[864,432]{1,0:T(8,128)(2,1)}, u32[]{:S(2)}) copy-start(bf16[864,432]{1,0:T(8,128)(2,1)} %constant.30.clone.dft_ref) | copy-start | bytes 2239492
  26.3 14.8 %copy-start.2 = (f32[432,128]{1,0:T(8,128)S(1)}, f32[432,128]{1,0:T(8,128)}, u32[]{:S(2)}) copy-start(f32[432,128]{1,0:T(8,128)} %constant.31.clone.cos_ref) | copy-start | bytes 663556
  26.3 14.8 %copy-start.3 = (f32[432,128]{1,0:T(8,128)S(1)}, f32[432,128]{1,0:T(8,128)}, u32[]{:S(2)}) copy-start(f32[432,128]{1,0:T(8,128)} %constant.32.clone.sin_ref) | copy-start | bytes 663556
  26.3 14.8 %copy-start.4 = (bf16[128,512]{1,0:T(8,128)(2,1)S(1)}, bf16[128,512]{1,0:T(8,128)(2,1)}, u32[]{:S(2)}) copy-start(bf16[128,512]{1,0:T(8,128)(2,1)} %constant.33.clone.join_ref) | copy-start | bytes 393220
  30.3 6.2 %collective-permute-start.5 = (bf16[272,128]{1,0:T(8,128)(2,1)S(1)}, bf16[272,128]{1,0:T(8,128)(2,1)S(1)}, u32[]{:S(2)}, u32[]{:S(2)}) collective-permute-start(bf16[272,128]{1,0:T(8,128)(2,1)S(1)} %get-tuple-element.19), channel_id=1, source_target_pairs={{0,12},{2,14},{4,8},{6,10},{8,4},{10,6},{12,0},{14,2},{1,13},{3,15... | collective-permute-start | bytes 208904 | tf_op jit(solution)/shard_map/ppermute | solution.py:440
  34.0 7.0 %collective-permute-start.6 = (bf16[272,128]{1,0:T(8,128)(2,1)S(1)}, bf16[272,128]{1,0:T(8,128)(2,1)S(1)}, u32[]{:S(2)}, u32[]{:S(2)}) collective-permute-start(bf16[272,128]{1,0:T(8,128)(2,1)S(1)} %get-tuple-element.20), channel_id=1, source_target_pairs={{0,14},{2,12},{4,10},{6,8},{8,6},{10,4},{12,2},{14,0},{1,15},{3,13... | collective-permute-start | bytes 208904 | tf_op jit(solution)/shard_map/ppermute | solution.py:440

commit v2 on v1

--- a/solution.py
+++ b/solution.py
@@ -204,7 +204,7 @@
 
 
 def section_one_kernel(plan, starts_ref, widths_ref, taps_ref, signal_ref, *rest):
-    (outs, (table, taps_rows, frames, total, sems)) = (rest[: plan.devices], rest[plan.devices :])
+    (outs, (taps_rows, frames, total, sems)) = (rest[: plan.devices], rest[plan.devices :])
     blocks, chan_len, live = (plan.blocks, plan.chan_len, plan.live)
     half = ROWS * live
     columns = 2 * half
@@ -249,36 +249,43 @@
         taps_rows[shift_index] = (
             pltpu.roll(flat, HOP * shift_index, axis=1) if shift_index else flat
         )
-    for piece in range(plan.depth // chan_len):
-        span = pl.ds(piece * chan_len, chan_len)
-        scale = jnp.concatenate(
-            [
-                jnp.broadcast_to(
-                    taps_rows[shift_index, :, span][None], (live // 8, 8, chan_len)
-                ).reshape(live, chan_len)
-                for shift_index in range(ROWS)
-            ],
-            axis=0,
-        )
-        for part in range(2):
-            table[pl.ds(part * half, half), span] = (
-                scale * rotation[part * half : (part + 1) * half]
-            ).astype(jnp.bfloat16)
-
-    for copy in copies:
-        copy.wait()
     count = 2 * plan.out_rows
     pairs = frames.reshape(blocks, 2 * (plan.local_rows + 2 * lead), LANES)
     acc = jnp.zeros((count, columns), jnp.float32)
-    for index in range(0, plan.depth // LANES, 2):
-        left = jnp.concatenate(
+    order = sorted(range(plan.depth // LANES), key=lambda index: (index % blocks, index // blocks))
+    turns = chan_len // LANES
+    batch = -(-blocks // 3)
+    arrived = 0
+    for piece in range(0, len(order), turns):
+        group = order[piece : piece + turns]
+        needed = max(index % blocks for index in group) // batch * batch + batch
+        while arrived < min(blocks, needed):
+            copies[arrived].wait()
+            arrived += 1
+        right = jnp.concatenate(
             [
-                pairs[(index + step) % blocks, pl.ds(2 * ((index + step) // blocks), count), :]
-                for step in range(2)
+                (
+                    jnp.concatenate(
+                        [
+                            jnp.broadcast_to(
+                                taps_rows[shift_index, :, pl.ds(index * LANES, LANES)][None],
+                                (live // 8, 8, LANES),
+                            ).reshape(live, LANES)
+                            for shift_index in range(ROWS)
+                        ]
+                        * 2,
+                        axis=0,
+                    )
+                    * rotation[:, index % turns * LANES : (index % turns + 1) * LANES]
+                ).astype(jnp.bfloat16)
+                for index in group
             ],
             axis=1,
         )
-        right = table[:, index * LANES : (index + 2) * LANES]
+        left = jnp.concatenate(
+            [pairs[index % blocks, pl.ds(2 * (index // blocks), count), :] for index in group],
+            axis=1,
+        )
         acc = acc + lax.dot_general(left, right, NT, preferred_element_type=jnp.float32)
     for tile in range(columns // LANES):
         total[tile] = acc[:, tile * LANES : (tile + 1) * LANES]
@@ -314,10 +321,32 @@
         ).astype(jnp.bfloat16)
 
 
+def fine_taps_kernel(plan, taps_ref, after_ref, out_ref):
+    lane = lax.broadcasted_iota(jnp.int32, (SLOT_LANES, LANES), 1)
+    row = lax.broadcasted_iota(jnp.int32, (SLOT_LANES, LANES), 0)
+    keep = lane // ROWS == row
+    source = lax.broadcasted_iota(jnp.int32, (2 * LANES, LANES), 0)
+    target = lax.broadcasted_iota(jnp.int32, (2 * LANES, LANES), 1)
+    spread = (source % ROWS == target % ROWS).astype(jnp.float32).astype(jnp.bfloat16)
+    for tap in range(plan.fine_taps):
+        (high, low) = ([], [])
+        for tile in range(plan.fine_rows // SLOT_LANES):
+            line = taps_ref[tap : tap + 1, tile * LANES : (tile + 1) * LANES]
+            part = jnp.where(keep, jnp.broadcast_to(line, (SLOT_LANES, LANES)), 0.0)
+            rounded = part.astype(jnp.bfloat16)
+            high.append(rounded)
+            low.append((part - rounded.astype(jnp.float32)).astype(jnp.bfloat16))
+        both = jnp.concatenate([jnp.concatenate(high, axis=0), jnp.concatenate(low, axis=0)], axis=1)
+        out_ref[tap] = lax.dot_general(
+            both, spread, (((1,), (0,)), ((), ())), preferred_element_type=jnp.float32
+        )
+
+
 def section_two_kernel(plan, widths_ref, taps_ref, dft_ref, cos_ref, sin_ref, join_ref, *rest):
     (blocks, out_ref, series) = (rest[: plan.devices], rest[plan.devices], rest[plan.devices + 1])
-    here = lax.axis_index("tm") * plan.zooms + lax.axis_index("zoom")
-    fine_rows = plan.fine_rows
+    (tm, zoom) = (lax.axis_index("tm"), lax.axis_index("zoom"))
+    here = tm * plan.zooms + zoom
+    (fine_rows, bins) = (plan.fine_rows, plan.bins)
     pad = 8
     series[...] = jnp.zeros_like(series)
     for step in range(plan.devices):
@@ -333,19 +362,95 @@
         (((1,), (0,)), ((), ())),
         preferred_element_type=jnp.float32,
     )
-    (even, odd) = (spun[:fine_rows], spun[fine_rows:])
     (cosine_tab, sine_tab) = (cos_ref[...], sin_ref[...])
     mixed = jnp.concatenate(
         [
             (part * factor).astype(jnp.bfloat16)
-            for part in (even, odd)
+            for part in (spun[:bins], spun[bins:])
             for factor in (cosine_tab, sine_tab)
         ],
         axis=1,
     )
-    out_ref[...] = lax.dot_general(
-        join_ref[...], mixed, NT, preferred_element_type=jnp.float32
-    )
+    joined = lax.dot_general(join_ref[...], mixed, NT, preferred_element_type=jnp.float32)
+
+    slots = LANES // SLOT_LANES
+    high = 2 * slots
+    flat = [jnp.zeros((high, LANES), jnp.float32)] * (-(-(ROWS * fine_rows) // LANES) + 2)
+    for turn in range(ROWS):
+        (first, offset) = divmod(turn * fine_rows, LANES)
+        piece = jnp.concatenate(
+            [joined[turn * high : (turn + 1) * high], jnp.zeros((high, LANES), jnp.float32)], axis=1
+        )
+        if offset:
+            piece = pltpu.roll(piece, offset, axis=1)
+        for tile in range(min(bins // LANES + 1, len(flat) - first)):
+            flat[first + tile] = flat[first + tile] + piece[:, tile * LANES : (tile + 1) * LANES]
+
+    row = lax.broadcasted_iota(jnp.int32, (high, LANES), 0)
+    lane = lax.broadcasted_iota(jnp.int32, (high, LANES), 1)
+    width = jnp.int32(0)
+    for band in range(plan.bands):
+        width = jnp.where(zoom == band, widths_ref[band], width)
+    slot = tm * CH_DEV + row % slots - 1
+    live = (slot < width).astype(jnp.float32)
+    upper_ok = (slot + 1 < width).astype(jnp.float32)
+    lower_ok = ((slot >= 1) & (slot < width)).astype(jnp.float32)
+    (lead, skew) = divmod(KEEP + EDGE, LANES)
+    below = jnp.where(
+        lane < LANES - skew,
+        pltpu.roll(flat[lead], LANES - skew, axis=1),
+        pltpu.roll(flat[lead + 1], LANES - skew, axis=1),
+    )
+    below = pltpu.roll(below, 1, axis=0)
+    (lead, skew) = divmod(KEEP - EDGE, LANES)
+    above = pltpu.roll(pltpu.roll(flat[0], skew, axis=1), high - 1, axis=0)
+    position = lane.astype(jnp.float32)
+    own = flat[1:]
+    span = -(-KEEP // LANES)
+    parts = []
+    for tile in range(span):
+        value = own[tile]
+        if tile == 0:
+            weight = (EDGE - 0.5 - position) * (0.5 / EDGE) * lower_ok
+            value = value * (1.0 - weight) + below * weight
+        if tile in (lead, lead + 1):
+            ramp = (position + (tile * LANES - (KEEP - EDGE) + 0.5)) * (0.5 / EDGE)
+            inside = lane >= skew if tile == lead else lane < skew
+            weight = jnp.where(inside, ramp * upper_ok, 0.0)
+            value = value * (1.0 - weight) + above * weight
+        value = value * live
+        if tile == span - 1:
+            value = jnp.where(lane < KEEP - tile * LANES, value, 0.0)
+        parts.append(value)
+    parts = [jnp.zeros_like(parts[0])] + parts + [jnp.zeros_like(parts[0])]
+
+    carry = [None, None]
+    for place in range(CH_DEV):
+        (first, offset) = divmod(place * KEEP, LANES)
+        (after, _) = divmod((place + 1) * KEEP, LANES)
+        last = place == CH_DEV - 1
+        count = after - first + 1
+        for part in range(2):
+            picked = part * slots + place + 1
+            tiles = []
+            for tile in range(count):
+                value = parts[tile + 1][part * slots : (part + 1) * slots]
+                if offset:
+                    before = parts[tile][part * slots : (part + 1) * slots]
+                    value = jnp.where(
+                        lane[:slots] < offset,
+                        pltpu.roll(before, offset, axis=1),
+                        pltpu.roll(value, offset, axis=1),
+                    )
+                tiles.append(value[picked % slots : picked % slots + 1])
+            if place:
+                tiles[0] = tiles[0] + carry[part]
+            carry[part] = tiles[-1]
+            if not last:
+                tiles = tiles[:-1]
+            line = jnp.concatenate(tiles, axis=1)
+            end = min(first * LANES + len(tiles) * LANES, CH_DEV * KEEP)
+            out_ref[part, :, first * LANES : end] = line[:, : end - first * LANES]
 
 
 def fine_tables(fine_rows):
@@ -353,7 +458,8 @@
     offset = KEEP // 2 + EDGE
     bins = np.arange(fine_rows) - offset
     spin = 2.0 * np.pi * (np.outer(bins, np.arange(fine_rows)) % fine_rows) / fine_rows
-    dft = np.concatenate([np.cos(spin), np.sin(spin)], axis=0)
+    margin = ((0, -fine_rows % LANES), (0, 0))
+    dft = np.concatenate([np.pad(np.cos(spin), margin), np.pad(np.sin(spin), margin)], axis=0)
     twist = 2.0 * np.pi * (np.outer(bins, np.arange(LANES) % ROWS) % fine_len) / fine_len
     join = np.zeros((ROWS, 2, LANES // SLOT_LANES, 4, LANES // SLOT_LANES, 2, ROWS))
     turn = 2.0 * np.pi * (np.outer(np.arange(ROWS), np.arange(ROWS)) % ROWS) / ROWS
@@ -370,8 +476,8 @@
         imag[:, 3, 0], imag[:, 3, 1] = (sine, -cosine)
     return (
         jnp.asarray(dft, jnp.bfloat16),
-        jnp.asarray(np.cos(twist), jnp.float32),
-        jnp.asarray(np.sin(twist), jnp.float32),
+        jnp.asarray(np.pad(np.cos(twist), margin), jnp.float32),
+        jnp.asarray(np.pad(np.sin(twist), margin), jnp.float32),
         jnp.asarray(join.reshape(LANES, 4 * LANES), jnp.bfloat16),
     )
 
@@ -394,6 +500,7 @@
         self.lead = -(-self.depth // self.row_len) - 1
         self.out_rows = self.local_rows + self.lead
         self.fine_rows = section2_shape[1] // ROWS
+        self.bins = -(-self.fine_rows // LANES) * LANES
 
     def fits(self, section2_shape):
         return (
@@ -408,6 +515,8 @@
             and (CH_DEV + 2) * SLOT_LANES <= LANES
             and self.out_rows % 16 == 0
             and self.fine_rows % 16 == 0
+            and EDGE == LANES
+            and KEEP + 2 * EDGE <= section2_shape[1]
             and section2_shape[1] % ROWS == 0
             and self.devices * self.samples == HOP * self.fine_taps * section2_shape[1]
         )
@@ -425,13 +534,12 @@
         in_specs=[smem, smem, vmem, pl.BlockSpec(memory_space=pl.ANY)],
         out_specs=[vmem] * plan.devices,
         scratch_shapes=[
-            pltpu.VMEM((columns, plan.depth), jnp.bfloat16),
             pltpu.VMEM((ROWS, 8, plan.depth), jnp.float32),
             pltpu.VMEM((plan.blocks, plan.local_rows + 2 * plan.lead, 2, LANES), jnp.bfloat16),
             pltpu.VMEM((columns // LANES, 2 * plan.out_rows, LANES), jnp.float32),
             pltpu.SemaphoreType.DMA((plan.blocks,)),
         ],
-        compiler_params=pltpu.CompilerParams(vmem_limit_bytes=40 * 2**20),
+        compiler_params=pltpu.CompilerParams(vmem_limit_bytes=62 * 2**20),
         name="section_one",
     )(band_starts, band_widths, section1_taps, signal)
     received = [sent[0]]
@@ -439,13 +547,18 @@
         pairs = [(index, index ^ step) for index in range(plan.devices)]
         received.append(lax.ppermute(sent[step], ("tm", "zoom"), pairs))
     fine_rows = plan.fine_rows
-    spread = jnp.tile(
-        section2_taps.reshape(plan.fine_taps, fine_rows, ROWS), (1, 1, LANES // ROWS)
-    )
+    spread = pl.pallas_call(
+        functools.partial(fine_taps_kernel, plan),
+        out_shape=jax.ShapeDtypeStruct((plan.fine_taps, fine_rows, LANES), jnp.float32),
+        in_specs=[vmem, pl.BlockSpec(memory_space=pl.ANY)],
+        out_specs=vmem,
+        compiler_params=pltpu.CompilerParams(vmem_limit_bytes=16 * 2**20),
+        name="fine_taps",
+    )(section2_taps, received[3])
     (dft, cosine_tab, sine_tab, join) = fine_tables(fine_rows)
-    bins = pl.pallas_call(
+    lines = pl.pallas_call(
         functools.partial(section_two_kernel, plan),
-        out_shape=jax.ShapeDtypeStruct((LANES, fine_rows), jnp.float32),
+        out_shape=jax.ShapeDtypeStruct((2, 1, CH_DEV * KEEP), jnp.float32),
         in_specs=[smem] + [vmem] * (5 + plan.devices),
         out_specs=vmem,
         scratch_shapes=[
@@ -454,22 +567,7 @@
         compiler_params=pltpu.CompilerParams(vmem_limit_bytes=24 * 2**20),
         name="section_two",
     )(band_widths, spread, dft, cosine_tab, sine_tab, join, *received)
-    slots = LANES // SLOT_LANES
-    whole = bins.reshape(ROWS, 2, slots, fine_rows).transpose(1, 2, 0, 3)
-    whole = whole.reshape(2, slots, 1, ROWS * fine_rows)
-    zoom = lax.axis_index("zoom")
-    band_width = jnp.sum(jnp.where(jnp.arange(plan.bands) == zoom, band_widths, 0))
-    slot_ids = lax.axis_index("tm") * CH_DEV + jnp.arange(CH_DEV, dtype=jnp.int32)
-    stitched = stitch_bands(
-        whole[:, 1 : CH_DEV + 1],
-        whole[:, 2 : CH_DEV + 2, :, :EDGE],
-        whole[:, :CH_DEV, :, KEEP + EDGE : KEEP + 2 * EDGE],
-        slot_ids,
-        band_width,
-        KEEP,
-        EDGE,
-    )
-    return stitched.reshape(1, 1, 2, 1, CH_DEV * KEEP)
+    return lines.reshape(1, 1, 2, 1, CH_DEV * KEEP)
 
 
 def solution(mesh):

time: 44.5 us -> 33.3 us (0.75)
  local copies, waits for them, and re-layouts: 11.4 us -> 0.9 us
  other arithmetic: 2.23 us -> 0 us
  waiting for transfers between devices: 5.2 us -> 6.79 us
    another operation x5 -> x0, local copies, waits for them, and re-layouts: 4.13 us -> none  [the longest x4 4.04 us: direct_plan(): jnp.tile(section2_taps.reshape(plan.fine_taps, fine_rows, ROWS), (1, 1, L...]
    unnamed x20 -> x14, local copies, waits for them, and re-layouts: 4.15 us -> 0.9 us
    mul x3 -> x0, local copies, waits for them, and re-layouts: 2.5 us -> none  [stitch_bands(): return joined * live]
    ppermute x7, waiting for transfers between devices: 5.2 us -> 6.79 us  [direct_plan(): received.append(lax.ppermute(sent[step], ('tm', 'zoom'), pairs))]
    convert_element_type x2 -> x0, other arithmetic: 1.3 us -> none  [the longest x1 0.65 us: stitch_bands(): (slot_ids + 1 < band_width).astype(jnp.float32)[None, :, None, None]]
    pallas_call x1, Pallas kernels: 11 us -> 9.81 us  [direct_plan(): pl.pallas_call(functools.partial(section_one_kernel, plan), out_shape=[bl...]
    pallas_call x1, Pallas kernels: 1.56 us -> 2.62 us  [direct_plan(): pl.pallas_call(functools.partial(section_two_kernel, plan), out_shape=jax...]
    reduce_sum x1 -> x0, other arithmetic: 0.63 us -> none  [direct_plan(): jnp.sum(jnp.where(jnp.arange(plan.bands) == zoom, band_widths, 0))]
  transfers between devices with their start and end apart: 7 -> 7, of which waited for: 2 -> 2; matrix products, arithmetic and copies ran while one was open for 18% -> 0% of each run, Pallas kernels for 0% -> 1%
where the time goes in v2:
time: 33.3 us; the launch traced here: 33.2 us
  Pallas kernels  12.9 us (39%)
  starting transfers between devices  12.5 us (38%)
  waiting for transfers between devices  6.79 us (20%)
  local copies, waits for them, and re-layouts  0.9 us (3%)
    ppermute x7, starting transfers between devices, direct_plan(): received.append(lax.ppermute(sent[step], ('tm', 'zoom'), pairs))  12.5 us
    pallas_call x1, Pallas kernels, direct_plan(): pl.pallas_call(functools.partial(section_one_kernel, plan), out_shape=[bl...  9.81 us
    ppermute x7, waiting for transfers between devices, direct_plan(): received.append(lax.ppermute(sent[step], ('tm', 'zoom'), pairs))  6.79 us
    pallas_call x1, Pallas kernels, direct_plan(): pl.pallas_call(functools.partial(section_two_kernel, plan), out_shape=jax...  2.62 us
    unnamed x14, local copies, waits for them, and re-layouts  0.9 us
  transfers between devices with their start and end apart: 7, of which 2 were waited for; matrix products, arithmetic and copies ran while one was open for 0% of the time, Pallas kernels for 1%

profile of v2, /device:TPU:0, one launch (start us, length us, event | category | flops | bytes accessed | tf_op | source)
XLA Modules:
  0.0 33.2 jit_solution(132267235368952616)
XLA Ops:
  0.0 0.0 copy-start.4
  0.0 9.8 %section_one.1 = (bf16[272,128]{1,0:T(8,128)(2,1)}, bf16[272,128]{1,0:T(8,128)(2,1)}, bf16[272,128]{1,0:T(8,128)(2,1)}, bf16[272,128]{1,0:T(8,128)(2,1)}, bf16[2...) custom-call(s32[2]{0:T(128)} %starts_ref.1, s32[2]{0:T(128)} %widths_ref.3, ...), custom_call_target="tpu_custom_call" | custom-call | tf_op jit(solution)/shard_map/section_one/pallas_call | solution.py:531
  9.8 4.0 %collective-permute-start = (bf16[272,128]{1,0:T(8,128)(2,1)}, bf16[272,128]{1,0:T(8,128)(2,1)S(1)}, u32[]{:S(2)}, u32[]{:S(2)}) collective-permute-start(bf16[272,128]{1,0:T(8,128)(2,1)} %get-tuple-element.13), channel_id=1, source_target_pairs={{0,6},{2,4},{4,2},{6,0},{8,14},{10,12},{12,10},{14,8},{1,7},{3,5},... | collective-permute-start | bytes 208904 | tf_op jit(solution)/shard_map/ppermute | solution.py:548
  13.9 0.5 %collective-permute-start.1 = (bf16[272,128]{1,0:T(8,128)(2,1)}, bf16[272,128]{1,0:T(8,128)(2,1)S(1)}, u32[]{:S(2)}, u32[]{:S(2)}) collective-permute-start(bf16[272,128]{1,0:T(8,128)(2,1)} %get-tuple-element.15), channel_id=1, source_target_pairs={{0,2},{2,0},{4,6},{6,4},{8,10},{10,8},{12,14},{14,12},{1,3},{3,1},... | collective-permute-start | bytes 208904 | tf_op jit(solution)/shard_map/ppermute | solution.py:548
  14.4 0.1 collective-permute-start.2
  14.5 2.9 %collective-permute-start.3 = (bf16[272,128]{1,0:T(8,128)(2,1)}, bf16[272,128]{1,0:T(8,128)(2,1)S(1)}, u32[]{:S(2)}, u32[]{:S(2)}) collective-permute-start(bf16[272,128]{1,0:T(8,128)(2,1)} %get-tuple-element.17), channel_id=1, source_target_pairs={{0,8},{2,10},{4,12},{6,14},{8,0},{10,2},{12,4},{14,6},{1,9},{3,11}... | collective-permute-start | bytes 208904 | tf_op jit(solution)/shard_map/ppermute | solution.py:548
  17.4 1.3 %collective-permute-start.4 = (bf16[272,128]{1,0:T(8,128)(2,1)}, bf16[272,128]{1,0:T(8,128)(2,1)S(1)}, u32[]{:S(2)}, u32[]{:S(2)}) collective-permute-start(bf16[272,128]{1,0:T(8,128)(2,1)} %get-tuple-element.18), channel_id=1, source_target_pairs={{0,10},{2,8},{4,14},{6,12},{8,2},{10,0},{12,6},{14,4},{1,11},{3,9}... | collective-permute-start | bytes 208904 | tf_op jit(solution)/shard_map/ppermute | solution.py:548
  18.7 0.0 collective-permute-done.after_ref.rest_3_
  18.7 3.6 %collective-permute-start.5 = (bf16[272,128]{1,0:T(8,128)(2,1)}, bf16[272,128]{1,0:T(8,128)(2,1)S(1)}, u32[]{:S(2)}, u32[]{:S(2)}) collective-permute-start(bf16[272,128]{1,0:T(8,128)(2,1)} %get-tuple-element.19), channel_id=1, source_target_pairs={{0,12},{2,14},{4,8},{6,10},{8,4},{10,6},{12,0},{14,2},{1,13},{3,15... | collective-permute-start | bytes 208904 | tf_op jit(solution)/shard_map/ppermute | solution.py:548
  22.3 0.0 collective-permute-done.1.rest_1_
  22.3 0.0 collective-permute-start.6
  22.4 0.0 copy-done.4
  22.4 0.5 %fine_taps.1.taps_ref = f32[5,432,128]{2,1,0:T(8,128)S(1)} custom-call(f32[5,3456]{1,0:T(8,128)S(1)} %copy-done.4, bf16[272,128]{1,0:T(8,128)(2,1)S(1)} %collective-permute-done.after_ref.rest_3_), custom_call_target="tpu_custom_call" | custom-call | tf_op jit(solution)/shard_map/fine_taps/pallas_call | solution.py:550
  22.8 0.0 collective-permute-done.2.rest_2_
  22.8 0.0 collective-permute-done.3.rest_4_
  22.8 5.5 %collective-permute-done.4.rest_5_ = bf16[272,128]{1,0:T(8,128)(2,1)S(1)} collective-permute-done((bf16[272,128]{1,0:T(8,128)(2,1)}, bf16[272,128]{1,0:T(8,128)(2,1)S(1)}, u32[]{:S(2)}, u32[]{:S(2)}) %collective-permute-start.4) | collective-permute-done | bytes 69664 | tf_op jit(solution)/shard_map/ppermute | solution.py:548
  28.4 0.0 collective-permute-done.5.rest_6_
  28.4 1.3 %collective-permute-done.6.rest_7_ = bf16[272,128]{1,0:T(8,128)(2,1)S(1)} collective-permute-done((bf16[272,128]{1,0:T(8,128)(2,1)}, bf16[272,128]{1,0:T(8,128)(2,1)S(1)}, u32[]{:S(2)}, u32[]{:S(2)}) %collective-permute-start.6) | collective-permute-done | bytes 69664 | tf_op jit(solution)/shard_map/ppermute | solution.py:548
  29.6 0.0 copy-done.3
  29.6 0.0 copy-done.1
  29.6 0.0 copy-done.2
  29.7 0.0 copy-start.5
  29.7 0.9 %copy-done.5 = bf16[272,128]{1,0:T(8,128)(2,1)S(1)} copy-done((bf16[272,128]{1,0:T(8,128)(2,1)S(1)}, bf16[272,128]{1,0:T(8,128)(2,1)}, u32[]{:S(2)}) %copy-start.5) | copy-done | bytes 69656
  30.5 2.6 %section_two.1 = f32[2,1,14580]{2,1,0:T(1,128)} custom-call(s32[2]{0:T(128)S(1)} %copy-done.6, f32[5,432,128]{2,1,0:T(8,128)S(1)} %fine_taps.1.taps_ref, bf16[1024,432]{1,0:T(8,128)(2,1)S(1)} %copy-done, f32[512,128]{1,0:T(8,128)S(1)} %copy-done.2, f32[512,128]{1,0:T(8,128)S(1)} %copy-done.1, bf16[128,512]{1,0:T(8,128)(2,1)S(1)} %copy-done.3, ...), custom_call_target="tpu_custom_call" | custom-call | tf_op jit(solution)/shard_map/section_two/pallas_call | solution.py:559
  (7 shorter events, 0.0 us)
Async XLA Ops:
  0.0 29.6 %copy-start.3 = (bf16[128,512]{1,0:T(8,128)(2,1)S(1)}, bf16[128,512]{1,0:T(8,128)(2,1)}, u32[]{:S(2)}) copy-start(bf16[128,512]{1,0:T(8,128)(2,1)} %constant.11.clone.join_ref) | copy-start | bytes 393220
  0.0 29.6 %copy-start.1 = (f32[512,128]{1,0:T(8,128)S(1)}, f32[512,128]{1,0:T(8,128)}, u32[]{:S(2)}) copy-start(f32[512,128]{1,0:T(8,128)} %constant.10.clone.sin_ref) | copy-start | bytes 786436
  0.0 29.6 %copy-start.2 = (f32[512,128]{1,0:T(8,128)S(1)}, f32[512,128]{1,0:T(8,128)}, u32[]{:S(2)}) copy-start(f32[512,128]{1,0:T(8,128)} %constant.9.clone.cos_ref) | copy-start | bytes 786436
  0.0 29.6 %copy-start = (bf16[1024,432]{1,0:T(8,128)(2,1)S(1)}, bf16[1024,432]{1,0:T(8,128)(2,1)}, u32[]{:S(2)}) copy-start(bf16[1024,432]{1,0:T(8,128)(2,1)} %constant.8.clone.dft_ref) | copy-start | bytes 2654212
  0.0 29.6 %copy-start.6 = (s32[2]{0:T(128)S(1)}, s32[2]{0:T(128)}, u32[]{:S(2)}) copy-start(s32[2]{0:T(128)} %widths_ref.3) | copy-start | bytes 28
  0.0 22.3 %copy-start.4 = (f32[5,3456]{1,0:T(8,128)S(1)}, f32[5,3456]{1,0:T(8,128)}, u32[]{:S(2)}) copy-start(f32[5,3456]{1,0:T(8,128)} %taps_ref.3) | copy-start | bytes 207364
  9.8 8.9 %collective-permute-start = (bf16[272,128]{1,0:T(8,128)(2,1)}, bf16[272,128]{1,0:T(8,128)(2,1)S(1)}, u32[]{:S(2)}, u32[]{:S(2)}) collective-permute-start(bf16[272,128]{1,0:T(8,128)(2,1)} %get-tuple-element.13), channel_id=1, source_target_pairs={{0,6},{2,4},{4,2},{6,0},{8,14},{10,12},{12,10},{14,8},{1,7},{3,5},... | collective-permute-start | bytes 208904 | tf_op jit(solution)/shard_map/ppermute | solution.py:548
  13.9 8.5 %collective-permute-start.1 = (bf16[272,128]{1,0:T(8,128)(2,1)}, bf16[272,128]{1,0:T(8,128)(2,1)S(1)}, u32[]{:S(2)}, u32[]{:S(2)}) collective-permute-start(bf16[272,128]{1,0:T(8,128)(2,1)} %get-tuple-element.15), channel_id=1, source_target_pairs={{0,2},{2,0},{4,6},{6,4},{8,10},{10,8},{12,14},{14,12},{1,3},{3,1},... | collective-permute-start | bytes 208904 | tf_op jit(solution)/shard_map/ppermute | solution.py:548
  14.4 8.4 %collective-permute-start.2 = (bf16[272,128]{1,0:T(8,128)(2,1)}, bf16[272,128]{1,0:T(8,128)(2,1)S(1)}, u32[]{:S(2)}, u32[]{:S(2)}) collective-permute-start(bf16[272,128]{1,0:T(8,128)(2,1)} %get-tuple-element.16), channel_id=1, source_target_pairs={{0,4},{2,6},{4,0},{6,2},{8,12},{10,14},{12,8},{14,10},{1,5},{3,7},... | collective-permute-start | bytes 208904 | tf_op jit(solution)/shard_map/ppermute | solution.py:548
  14.5 8.3 %collective-permute-start.3 = (bf16[272,128]{1,0:T(8,128)(2,1)}, bf16[272,128]{1,0:T(8,128)(2,1)S(1)}, u32[]{:S(2)}, u32[]{:S(2)}) collective-permute-start(bf16[272,128]{1,0:T(8,128)(2,1)} %get-tuple-element.17), channel_id=1, source_target_pairs={{0,8},{2,10},{4,12},{6,14},{8,0},{10,2},{12,4},{14,6},{1,9},{3,11}... | collective-permute-start | bytes 208904 | tf_op jit(solution)/shard_map/ppermute | solution.py:548
  17.4 10.9 %collective-permute-start.4 = (bf16[272,128]{1,0:T(8,128)(2,1)}, bf16[272,128]{1,0:T(8,128)(2,1)S(1)}, u32[]{:S(2)}, u32[]{:S(2)}) collective-permute-start(bf16[272,128]{1,0:T(8,128)(2,1)} %get-tuple-element.18), channel_id=1, source_target_pairs={{0,10},{2,8},{4,14},{6,12},{8,2},{10,0},{12,6},{14,4},{1,11},{3,9}... | collective-permute-start | bytes 208904 | tf_op jit(solution)/shard_map/ppermute | solution.py:548
  18.7 9.7 %collective-permute-start.5 = (bf16[272,128]{1,0:T(8,128)(2,1)}, bf16[272,128]{1,0:T(8,128)(2,1)S(1)}, u32[]{:S(2)}, u32[]{:S(2)}) collective-permute-start(bf16[272,128]{1,0:T(8,128)(2,1)} %get-tuple-element.19), channel_id=1, source_target_pairs={{0,12},{2,14},{4,8},{6,10},{8,4},{10,6},{12,0},{14,2},{1,13},{3,15... | collective-permute-start | bytes 208904 | tf_op jit(solution)/shard_map/ppermute | solution.py:548
  22.3 7.3 %collective-permute-start.6 = (bf16[272,128]{1,0:T(8,128)(2,1)}, bf16[272,128]{1,0:T(8,128)(2,1)S(1)}, u32[]{:S(2)}, u32[]{:S(2)}) collective-permute-start(bf16[272,128]{1,0:T(8,128)(2,1)} %get-tuple-element.20), channel_id=1, source_target_pairs={{0,14},{2,12},{4,10},{6,8},{8,6},{10,4},{12,2},{14,0},{1,15},{3,13... | collective-permute-start | bytes 208904 | tf_op jit(solution)/shard_map/ppermute | solution.py:548
  29.7 0.9 %copy-start.5 = (bf16[272,128]{1,0:T(8,128)(2,1)S(1)}, bf16[272,128]{1,0:T(8,128)(2,1)}, u32[]{:S(2)}) copy-start(bf16[272,128]{1,0:T(8,128)(2,1)} %get-tuple-element.14.rest_0_) | copy-start | bytes 208900

commit v3 on v2

--- a/solution.py
+++ b/solution.py
@@ -192,6 +192,7 @@
 ROWS = 8
 LANES = 128
 SLOT_LANES = 2 * ROWS
+PAD = 8
 NT = (((1,), (1,)), ((), ()))
 
 
@@ -203,8 +204,20 @@
     return (total * square + 1.5707963267949) * value
 
 
-def section_one_kernel(plan, starts_ref, widths_ref, taps_ref, signal_ref, *rest):
-    (outs, (taps_rows, frames, total, sems)) = (rest[: plan.devices], rest[plan.devices :])
+def section_one_kernel(plan, starts_hbm, widths_hbm, taps_hbm, signal_ref, *rest):
+    (outs, (width_ref, taps_rows, frames, total, *rest)) = (
+        rest[: plan.devices],
+        rest[plan.devices :],
+    )
+    (starts_ref, widths_ref, taps_ref, small_sems, sems) = rest
+    small = [
+        pltpu.make_async_copy(source, target, small_sems.at[index])
+        for index, (source, target) in enumerate(
+            [(starts_hbm, starts_ref), (widths_hbm, widths_ref), (taps_hbm, taps_ref)]
+        )
+    ]
+    for copy in small:
+        copy.start()
     blocks, chan_len, live = (plan.blocks, plan.chan_len, plan.live)
     half = ROWS * live
     columns = 2 * half
@@ -216,11 +229,13 @@
         for block in range(blocks)
     ]
     for copy in copies:
-        copy.start()
+        copy.start(priority=1)
     edge = jnp.zeros((blocks, lead, 2, LANES), jnp.bfloat16)
     frames[:, :lead] = edge
     frames[:, lead + plan.local_rows :] = edge
 
+    for copy in small:
+        copy.wait()
     row = lax.broadcasted_iota(jnp.int32, (columns, 1), 0)
     imag = (row >= half).astype(jnp.int32)
     shift = (row - imag * half) // live
@@ -300,12 +315,16 @@
     sign = jnp.where(lane < half, -1.0, 1.0)
     coarse = (real_rows + sign * pltpu.roll(imag_rows, half, axis=1)).astype(jnp.bfloat16)
 
-    here = lax.axis_index("tm") * plan.zooms + lax.axis_index("zoom")
+    (tm, zoom) = (lax.axis_index("tm"), lax.axis_index("zoom"))
+    mine = jnp.int32(0)
+    for band in range(plan.bands):
+        mine = jnp.where(zoom == band, widths_ref[band], mine)
+    width_ref[...] = jnp.broadcast_to(mine, width_ref.shape)
     code = ident * SLOT_LANES + imag * ROWS + shift
     out_lane = lax.broadcasted_iota(jnp.int32, (1, LANES), 1)
     slot = out_lane // SLOT_LANES
     for step in range(plan.devices):
-        target = jnp.bitwise_xor(here, step)
+        target = jnp.bitwise_xor(tm * plan.zooms + zoom, step)
         (target_tm, target_zoom) = (target // plan.zooms, target % plan.zooms)
         (band_first, width) = (jnp.int32(0), jnp.int32(0))
         for band in range(plan.bands):
@@ -337,25 +356,42 @@
             high.append(rounded)
             low.append((part - rounded.astype(jnp.float32)).astype(jnp.bfloat16))
         both = jnp.concatenate([jnp.concatenate(high, axis=0), jnp.concatenate(low, axis=0)], axis=1)
-        out_ref[tap] = lax.dot_general(
+        out_ref[pl.ds(PAD + tap * plan.fine_rows, plan.fine_rows), :] = lax.dot_general(
             both, spread, (((1,), (0,)), ((), ())), preferred_element_type=jnp.float32
         )
-
-
-def section_two_kernel(plan, widths_ref, taps_ref, dft_ref, cos_ref, sin_ref, join_ref, *rest):
-    (blocks, out_ref, series) = (rest[: plan.devices], rest[plan.devices], rest[plan.devices + 1])
-    (tm, zoom) = (lax.axis_index("tm"), lax.axis_index("zoom"))
-    here = tm * plan.zooms + zoom
+    out_ref[:PAD] = jnp.zeros((PAD, LANES), jnp.float32)
+
+
+def add_blocks(plan, steps, taps_ref, blocks, sums):
+    here = lax.axis_index("tm") * plan.zooms + lax.axis_index("zoom")
+    (fine_rows, out_rows) = (plan.fine_rows, plan.out_rows)
+    sums[...] = jnp.zeros_like(sums)
+    for step, block in zip(steps, blocks):
+        start = jnp.bitwise_xor(here, step) * plan.local_rows + (PAD - plan.lead)
+        goal = pl.ds(lax.rem(start + (fine_rows - PAD), fine_rows), out_rows)
+        scale = taps_ref[pl.ds(start, out_rows), :]
+        sums[goal, :] += scale * block[...].astype(jnp.float32)
+    return jnp.concatenate(
+        [
+            sums[:out_rows] + sums[fine_rows : fine_rows + out_rows],
+            sums[out_rows:fine_rows],
+        ],
+        axis=0,
+    )
+
+
+def merge_kernel(plan, steps, taps_ref, *rest):
+    (blocks, (kept_ref, sums)) = (rest[: len(steps)], rest[len(steps) :])
+    kept_ref[...] = add_blocks(plan, steps, taps_ref, blocks, sums)
+
+
+def section_two_kernel(
+    plan, steps, width_ref, kept_ref, taps_ref, dft_ref, cos_ref, sin_ref, join_ref, *rest
+):
+    (blocks, (out_ref, sums)) = (rest[: len(steps)], rest[len(steps) :])
+    tm = lax.axis_index("tm")
     (fine_rows, bins) = (plan.fine_rows, plan.bins)
-    pad = 8
-    series[...] = jnp.zeros_like(series)
-    for step in range(plan.devices):
-        source = jnp.bitwise_xor(here, step)
-        span = pl.ds(source * plan.local_rows + (pad - plan.lead), plan.out_rows)
-        series[span, :] += blocks[step][...].astype(jnp.float32)
-    fine_in = jnp.zeros((fine_rows, LANES), jnp.float32)
-    for tap in range(plan.fine_taps):
-        fine_in = fine_in + taps_ref[tap] * series[pl.ds(pad + tap * fine_rows, fine_rows), :]
+    fine_in = kept_ref[...] + add_blocks(plan, steps, taps_ref, blocks, sums)
     spun = lax.dot_general(
         dft_ref[...],
         fine_in.astype(jnp.bfloat16),
@@ -388,9 +424,7 @@
 
     row = lax.broadcasted_iota(jnp.int32, (high, LANES), 0)
     lane = lax.broadcasted_iota(jnp.int32, (high, LANES), 1)
-    width = jnp.int32(0)
-    for band in range(plan.bands):
-        width = jnp.where(zoom == band, widths_ref[band], width)
+    width = width_ref[0:1, :]
     slot = tm * CH_DEV + row % slots - 1
     live = (slot < width).astype(jnp.float32)
     upper_ok = (slot + 1 < width).astype(jnp.float32)
@@ -513,6 +547,9 @@
             and (2 * ROWS * self.live) % LANES == 0
             and 2 * ROWS * self.live <= 4 * LANES
             and (CH_DEV + 2) * SLOT_LANES <= LANES
+            and self.devices >= 4
+            and self.lead <= PAD
+            and self.out_rows <= self.fine_rows
             and self.out_rows % 16 == 0
             and self.fine_rows % 16 == 0
             and EDGE == LANES
@@ -524,49 +561,76 @@
 
 def direct_plan(plan, voltages, section1_taps, section2_taps, band_starts, band_widths):
     signal = voltages[0].reshape(2, plan.local_rows, plan.blocks, LANES).transpose(1, 2, 0, 3)
-    smem = pl.BlockSpec(memory_space=pltpu.SMEM)
+    far = [
+        pltpu.with_memory_space_constraint(array, pltpu.HBM)
+        for array in (band_starts, band_widths, section1_taps, signal)
+    ]
     vmem = pl.BlockSpec(memory_space=pltpu.VMEM)
     columns = 2 * ROWS * plan.live
     block = jax.ShapeDtypeStruct((plan.out_rows, LANES), jnp.bfloat16)
-    sent = pl.pallas_call(
+    (*sent, width) = pl.pallas_call(
         functools.partial(section_one_kernel, plan),
-        out_shape=[block] * plan.devices,
-        in_specs=[smem, smem, vmem, pl.BlockSpec(memory_space=pl.ANY)],
-        out_specs=[vmem] * plan.devices,
+        out_shape=[block] * plan.devices + [jax.ShapeDtypeStruct((8, LANES), jnp.int32)],
+        in_specs=[pl.BlockSpec(memory_space=pltpu.HBM)] * 4,
+        out_specs=[vmem] * (plan.devices + 1),
         scratch_shapes=[
             pltpu.VMEM((ROWS, 8, plan.depth), jnp.float32),
             pltpu.VMEM((plan.blocks, plan.local_rows + 2 * plan.lead, 2, LANES), jnp.bfloat16),
             pltpu.VMEM((columns // LANES, 2 * plan.out_rows, LANES), jnp.float32),
+            pltpu.SMEM((plan.bands,), jnp.int32),
+            pltpu.SMEM((plan.bands,), jnp.int32),
+            pltpu.VMEM((plan.taps, plan.chan_len), jnp.float32),
+            pltpu.SemaphoreType.DMA((3,)),
             pltpu.SemaphoreType.DMA((plan.blocks,)),
         ],
-        compiler_params=pltpu.CompilerParams(vmem_limit_bytes=62 * 2**20),
+        compiler_params=pltpu.CompilerParams(vmem_limit_bytes=40 * 2**20),
         name="section_one",
-    )(band_starts, band_widths, section1_taps, signal)
-    received = [sent[0]]
-    for step in range(1, plan.devices):
+    )(*far)
+    order = list(range(plan.devices - 1, 0, -1))
+    received = {0: sent[0]}
+    for step in order:
         pairs = [(index, index ^ step) for index in range(plan.devices)]
-        received.append(lax.ppermute(sent[step], ("tm", "zoom"), pairs))
+        received[step] = lax.ppermute(sent[step], ("tm", "zoom"), pairs)
+    split = len(order) // 2 + 1
+    (early, late) = ([0] + order[:split], order[split:])
     fine_rows = plan.fine_rows
     spread = pl.pallas_call(
         functools.partial(fine_taps_kernel, plan),
-        out_shape=jax.ShapeDtypeStruct((plan.fine_taps, fine_rows, LANES), jnp.float32),
+        out_shape=jax.ShapeDtypeStruct((PAD + plan.fine_taps * fine_rows, LANES), jnp.float32),
         in_specs=[vmem, pl.BlockSpec(memory_space=pl.ANY)],
         out_specs=vmem,
         compiler_params=pltpu.CompilerParams(vmem_limit_bytes=16 * 2**20),
         name="fine_taps",
-    )(section2_taps, received[3])
+    )(section2_taps, received[order[1]])
+    sums = pltpu.VMEM((fine_rows + plan.out_rows, LANES), jnp.float32)
+    kept = pl.pallas_call(
+        functools.partial(merge_kernel, plan, early),
+        out_shape=jax.ShapeDtypeStruct((fine_rows, LANES), jnp.float32),
+        in_specs=[vmem] * (1 + len(early)),
+        out_specs=vmem,
+        scratch_shapes=[sums],
+        compiler_params=pltpu.CompilerParams(vmem_limit_bytes=16 * 2**20),
+        name="merge",
+    )(spread, *[received[step] for step in early])
     (dft, cosine_tab, sine_tab, join) = fine_tables(fine_rows)
     lines = pl.pallas_call(
-        functools.partial(section_two_kernel, plan),
+        functools.partial(section_two_kernel, plan, late),
         out_shape=jax.ShapeDtypeStruct((2, 1, CH_DEV * KEEP), jnp.float32),
-        in_specs=[smem] + [vmem] * (5 + plan.devices),
+        in_specs=[vmem] * (7 + len(late)),
         out_specs=vmem,
-        scratch_shapes=[
-            pltpu.VMEM((plan.fine_taps * fine_rows + 16 + plan.lead, LANES), jnp.float32)
-        ],
+        scratch_shapes=[sums],
         compiler_params=pltpu.CompilerParams(vmem_limit_bytes=24 * 2**20),
         name="section_two",
-    )(band_widths, spread, dft, cosine_tab, sine_tab, join, *received)
+    )(
+        width,
+        kept,
+        spread,
+        dft,
+        cosine_tab,
+        sine_tab,
+        join,
+        *[received[step] for step in late],
+    )
     return lines.reshape(1, 1, 2, 1, CH_DEV * KEEP)
 
 

time: 33.3 us -> 29.2 us (0.88)
  waiting for transfers between devices: 6.79 us -> 3.18 us
  starting transfers between devices: 12.5 us -> 13.9 us
  Pallas kernels: 12.9 us -> 11.7 us
  local copies, waits for them, and re-layouts: 0.9 us -> 0.02 us
    ppermute x7, waiting for transfers between devices: 6.79 us -> 3.18 us  [direct_plan(): received[step] = lax.ppermute(sent[step], ('tm', 'zoom'), pairs)]
    ppermute x7, starting transfers between devices: 12.5 us -> 13.9 us  [direct_plan(): received[step] = lax.ppermute(sent[step], ('tm', 'zoom'), pairs)]
    unnamed x14 -> x10, local copies, waits for them, and re-layouts: 0.9 us -> 0.02 us
    pallas_call x1, Pallas kernels: 9.81 us -> 9.17 us  [direct_plan(): pl.pallas_call(functools.partial(section_one_kernel, plan), out_shape=[bl...]
    pallas_call x1 -> x2, Pallas kernels: 2.62 us -> 2.07 us  [the longest x1 1.92 us: direct_plan(): pl.pallas_call(functools.partial(section_two_kernel, plan, late), out_sha...]
  transfers between devices with their start and end apart: 7 -> 7, of which waited for: 2 -> 3; matrix products, arithmetic and copies ran while one was open for 0% -> 0% of each run, Pallas kernels for 1% -> 2%
where the time goes in v3:
time: 29.2 us; the launch traced here: 28.9 us
  starting transfers between devices  13.9 us (48%)
  Pallas kernels  11.7 us (40%)
  waiting for transfers between devices  3.18 us (11%)
    ppermute x7, starting transfers between devices, direct_plan(): received[step] = lax.ppermute(sent[step], ('tm', 'zoom'), pairs)  13.9 us
    pallas_call x1, Pallas kernels, direct_plan(): pl.pallas_call(functools.partial(section_one_kernel, plan), out_shape=[bl...  9.17 us
    ppermute x7, waiting for transfers between devices, direct_plan(): received[step] = lax.ppermute(sent[step], ('tm', 'zoom'), pairs)  3.18 us
    pallas_call x1, Pallas kernels, direct_plan(): pl.pallas_call(functools.partial(section_two_kernel, plan, late), out_sha...  1.92 us
  transfers between devices with their start and end apart: 7, of which 3 were waited for; matrix products, arithmetic and copies ran while one was open for 0% of the time, Pallas kernels for 2%

profile of v3, /device:TPU:0, one launch (start us, length us, event | category | flops | bytes accessed | tf_op | source)
XLA Modules:
  0.0 28.9 jit_solution(3497653421226852)
XLA Ops:
  0.0 0.0 copy-start.3
  0.0 9.2 %section_one.1 = (bf16[272,128]{1,0:T(8,128)(2,1)S(1)}, bf16[272,128]{1,0:T(8,128)(2,1)S(1)}, bf16[272,128]{1,0:T(8,128)(2,1)S(1)}, bf16[272,128]{1,0:T(8,128)(2...) custom-call(s32[2]{0:T(128)} %starts_hbm.1, ...), custom_call_target="tpu_custom_call" | custom-call | tf_op jit(solution)/shard_map/section_one/pallas_call | solution.py:571
  9.2 5.1 %collective-permute-start = (bf16[272,128]{1,0:T(8,128)(2,1)S(1)}, bf16[272,128]{1,0:T(8,128)(2,1)S(1)}, u32[]{:S(2)}, u32[]{:S(2)}) collective-permute-start(bf16[272,128]{1,0:T(8,128)(2,1)S(1)} %get-tuple-element.15), channel_id=1, source_target_pairs={{0,12},{2,14},{4,8},{6,10},{8,4},{10,6},{12,0},{14,2},{1,13},{3,15... | collective-permute-start | bytes 208904 | tf_op jit(solution)/shard_map/ppermute | solution.py:593
  14.3 1.1 %collective-permute-start.1 = (bf16[272,128]{1,0:T(8,128)(2,1)S(1)}, bf16[272,128]{1,0:T(8,128)(2,1)S(1)}, u32[]{:S(2)}, u32[]{:S(2)}) collective-permute-start(bf16[272,128]{1,0:T(8,128)(2,1)S(1)} %get-tuple-element.17), channel_id=1, source_target_pairs={{0,14},{2,12},{4,10},{6,8},{8,6},{10,4},{12,2},{14,0},{1,15},{3,13... | collective-permute-start | bytes 208904 | tf_op jit(solution)/shard_map/ppermute | solution.py:593
  15.5 0.8 %collective-permute-start.2 = (bf16[272,128]{1,0:T(8,128)(2,1)S(1)}, bf16[272,128]{1,0:T(8,128)(2,1)S(1)}, u32[]{:S(2)}, u32[]{:S(2)}) collective-permute-start(bf16[272,128]{1,0:T(8,128)(2,1)S(1)} %get-tuple-element.18), channel_id=1, source_target_pairs={{0,10},{2,8},{4,14},{6,12},{8,2},{10,0},{12,6},{14,4},{1,11},{3,9}... | collective-permute-start | bytes 208904 | tf_op jit(solution)/shard_map/ppermute | solution.py:593
  16.2 2.0 %collective-permute-start.3 = (bf16[272,128]{1,0:T(8,128)(2,1)S(1)}, bf16[272,128]{1,0:T(8,128)(2,1)S(1)}, u32[]{:S(2)}, u32[]{:S(2)}) collective-permute-start(bf16[272,128]{1,0:T(8,128)(2,1)S(1)} %get-tuple-element.19), channel_id=1, source_target_pairs={{0,8},{2,10},{4,12},{6,14},{8,0},{10,2},{12,4},{14,6},{1,9},{3,11}... | collective-permute-start | bytes 208904 | tf_op jit(solution)/shard_map/ppermute | solution.py:593
  18.2 2.3 %collective-permute-start.4 = (bf16[272,128]{1,0:T(8,128)(2,1)S(1)}, bf16[272,128]{1,0:T(8,128)(2,1)S(1)}, u32[]{:S(2)}, u32[]{:S(2)}) collective-permute-start(bf16[272,128]{1,0:T(8,128)(2,1)S(1)} %get-tuple-element.20), channel_id=1, source_target_pairs={{0,6},{2,4},{4,2},{6,0},{8,14},{10,12},{12,10},{14,8},{1,7},{3,5},... | collective-permute-start | bytes 208904 | tf_op jit(solution)/shard_map/ppermute | solution.py:593
  20.5 0.0 collective-permute-done.after_ref.rest_2_
  20.6 1.3 %collective-permute-start.5 = (bf16[272,128]{1,0:T(8,128)(2,1)S(1)}, bf16[272,128]{1,0:T(8,128)(2,1)S(1)}, u32[]{:S(2)}, u32[]{:S(2)}) collective-permute-start(bf16[272,128]{1,0:T(8,128)(2,1)S(1)} %get-tuple-element.21), channel_id=1, source_target_pairs={{0,4},{2,6},{4,0},{6,2},{8,12},{10,14},{12,8},{14,10},{1,5},{3,7},... | collective-permute-start | bytes 208904 | tf_op jit(solution)/shard_map/ppermute | solution.py:593
  21.9 0.0 collective-permute-done.1.rest_1_
  21.9 1.2 %collective-permute-start.6 = (bf16[272,128]{1,0:T(8,128)(2,1)S(1)}, bf16[272,128]{1,0:T(8,128)(2,1)S(1)}, u32[]{:S(2)}, u32[]{:S(2)}) collective-permute-start(bf16[272,128]{1,0:T(8,128)(2,1)S(1)} %get-tuple-element.22), channel_id=1, source_target_pairs={{0,2},{2,0},{4,6},{6,4},{8,10},{10,8},{12,14},{14,12},{1,3},{3,1},... | collective-permute-start | bytes 208904 | tf_op jit(solution)/shard_map/ppermute | solution.py:593
  23.1 0.0 copy-done.4
  23.1 0.5 %fine_taps.1.taps_ref = f32[2168,128]{1,0:T(8,128)S(1)} custom-call(f32[5,3456]{1,0:T(8,128)S(1)} %copy-done.4, bf16[272,128]{1,0:T(8,128)(2,1)S(1)} %collective-permute-done.after_ref.rest_2_), custom_call_target="tpu_custom_call" | custom-call | tf_op jit(solution)/shard_map/fine_taps/pallas_call | solution.py:597
  23.6 2.5 %collective-permute-done.2.rest_3_ = bf16[272,128]{1,0:T(8,128)(2,1)S(1)} collective-permute-done((bf16[272,128]{1,0:T(8,128)(2,1)S(1)}, bf16[272,128]{1,0:T(8,128)(2,1)S(1)}, u32[]{:S(2)}, u32[]{:S(2)}) %collective-permute-start.2) | collective-permute-done | bytes 69664 | tf_op jit(solution)/shard_map/ppermute | solution.py:593
  26.1 0.2 collective-permute-done.3.rest_4_
  26.3 0.1 merge.1.kept_ref
  26.4 0.0 collective-permute-done.4.rest_0_
  26.4 0.5 %collective-permute-done.5.rest_1_ = bf16[272,128]{1,0:T(8,128)(2,1)S(1)} collective-permute-done((bf16[272,128]{1,0:T(8,128)(2,1)S(1)}, bf16[272,128]{1,0:T(8,128)(2,1)S(1)}, u32[]{:S(2)}, u32[]{:S(2)}) %collective-permute-start.5) | collective-permute-done | bytes 69664 | tf_op jit(solution)/shard_map/ppermute | solution.py:593
  26.9 0.0 collective-permute-done.6.rest_2_
  26.9 0.0 copy-done.3
  26.9 0.0 copy-done.1
  26.9 0.0 copy-done.2
  26.9 0.0 copy-done
  26.9 1.9 %section_two.1 = f32[2,1,14580]{2,1,0:T(1,128)} custom-call(s32[8,128]{1,0:T(8,128)S(1)} %get-tuple-element.14.width_ref, f32[432,128]{1,0:T(8,128)S(1)} %merge.1.kept_ref, f32[2168,128]{1,0:T(8,128)S(1)} %fine_taps.1.taps_ref, bf16[1024,432]{1,0:T(8,128)(2,1)S(1)} %copy-done, f32[512,128]{1,0:T(8,128)S(1)} %copy-done.2, f32[512,128]{1,0:T(8,128)S(1)} %copy-done.1, ...), custom_call_target="tpu_custom_call" | custom-call | tf_op jit(solution)/shard_map/section_two/pallas_call | solution.py:616
  (4 shorter events, 0.0 us)
Async XLA Ops:
  0.0 26.9 %copy-start.3 = (bf16[128,512]{1,0:T(8,128)(2,1)S(1)}, bf16[128,512]{1,0:T(8,128)(2,1)}, u32[]{:S(2)}) copy-start(bf16[128,512]{1,0:T(8,128)(2,1)} %constant.11.clone.join_ref) | copy-start | bytes 393220
  0.0 26.9 %copy-start.1 = (f32[512,128]{1,0:T(8,128)S(1)}, f32[512,128]{1,0:T(8,128)}, u32[]{:S(2)}) copy-start(f32[512,128]{1,0:T(8,128)} %constant.10.clone.sin_ref) | copy-start | bytes 786436
  0.0 26.9 %copy-start.2 = (f32[512,128]{1,0:T(8,128)S(1)}, f32[512,128]{1,0:T(8,128)}, u32[]{:S(2)}) copy-start(f32[512,128]{1,0:T(8,128)} %constant.9.clone.cos_ref) | copy-start | bytes 786436
  0.0 26.9 %copy-start = (bf16[1024,432]{1,0:T(8,128)(2,1)S(1)}, bf16[1024,432]{1,0:T(8,128)(2,1)}, u32[]{:S(2)}) copy-start(bf16[1024,432]{1,0:T(8,128)(2,1)} %constant.8.clone.dft_ref) | copy-start | bytes 2654212
  0.0 23.1 %copy-start.4 = (f32[5,3456]{1,0:T(8,128)S(1)}, f32[5,3456]{1,0:T(8,128)}, u32[]{:S(2)}) copy-start(f32[5,3456]{1,0:T(8,128)} %taps_ref.1) | copy-start | bytes 207364
  9.2 11.4 %collective-permute-start = (bf16[272,128]{1,0:T(8,128)(2,1)S(1)}, bf16[272,128]{1,0:T(8,128)(2,1)S(1)}, u32[]{:S(2)}, u32[]{:S(2)}) collective-permute-start(bf16[272,128]{1,0:T(8,128)(2,1)S(1)} %get-tuple-element.15), channel_id=1, source_target_pairs={{0,12},{2,14},{4,8},{6,10},{8,4},{10,6},{12,0},{14,2},{1,13},{3,15... | collective-permute-start | bytes 208904 | tf_op jit(solution)/shard_map/ppermute | solution.py:593
  14.3 7.5 %collective-permute-start.1 = (bf16[272,128]{1,0:T(8,128)(2,1)S(1)}, bf16[272,128]{1,0:T(8,128)(2,1)S(1)}, u32[]{:S(2)}, u32[]{:S(2)}) collective-permute-start(bf16[272,128]{1,0:T(8,128)(2,1)S(1)} %get-tuple-element.17), channel_id=1, source_target_pairs={{0,14},{2,12},{4,10},{6,8},{8,6},{10,4},{12,2},{14,0},{1,15},{3,13... | collective-permute-start | bytes 208904 | tf_op jit(solution)/shard_map/ppermute | solution.py:593
  15.5 10.6 %collective-permute-start.2 = (bf16[272,128]{1,0:T(8,128)(2,1)S(1)}, bf16[272,128]{1,0:T(8,128)(2,1)S(1)}, u32[]{:S(2)}, u32[]{:S(2)}) collective-permute-start(bf16[272,128]{1,0:T(8,128)(2,1)S(1)} %get-tuple-element.18), channel_id=1, source_target_pairs={{0,10},{2,8},{4,14},{6,12},{8,2},{10,0},{12,6},{14,4},{1,11},{3,9}... | collective-permute-start | bytes 208904 | tf_op jit(solution)/shard_map/ppermute | solution.py:593
  16.2 10.0 %collective-permute-start.3 = (bf16[272,128]{1,0:T(8,128)(2,1)S(1)}, bf16[272,128]{1,0:T(8,128)(2,1)S(1)}, u32[]{:S(2)}, u32[]{:S(2)}) collective-permute-start(bf16[272,128]{1,0:T(8,128)(2,1)S(1)} %get-tuple-element.19), channel_id=1, source_target_pairs={{0,8},{2,10},{4,12},{6,14},{8,0},{10,2},{12,4},{14,6},{1,9},{3,11}... | collective-permute-start | bytes 208904 | tf_op jit(solution)/shard_map/ppermute | solution.py:593
  18.2 8.2 %collective-permute-start.4 = (bf16[272,128]{1,0:T(8,128)(2,1)S(1)}, bf16[272,128]{1,0:T(8,128)(2,1)S(1)}, u32[]{:S(2)}, u32[]{:S(2)}) collective-permute-start(bf16[272,128]{1,0:T(8,128)(2,1)S(1)} %get-tuple-element.20), channel_id=1, source_target_pairs={{0,6},{2,4},{4,2},{6,0},{8,14},{10,12},{12,10},{14,8},{1,7},{3,5},... | collective-permute-start | bytes 208904 | tf_op jit(solution)/shard_map/ppermute | solution.py:593
  20.6 6.3 %collective-permute-start.5 = (bf16[272,128]{1,0:T(8,128)(2,1)S(1)}, bf16[272,128]{1,0:T(8,128)(2,1)S(1)}, u32[]{:S(2)}, u32[]{:S(2)}) collective-permute-start(bf16[272,128]{1,0:T(8,128)(2,1)S(1)} %get-tuple-element.21), channel_id=1, source_target_pairs={{0,4},{2,6},{4,0},{6,2},{8,12},{10,14},{12,8},{14,10},{1,5},{3,7},... | collective-permute-start | bytes 208904 | tf_op jit(solution)/shard_map/ppermute | solution.py:593
  21.9 5.0 %collective-permute-start.6 = (bf16[272,128]{1,0:T(8,128)(2,1)S(1)}, bf16[272,128]{1,0:T(8,128)(2,1)S(1)}, u32[]{:S(2)}, u32[]{:S(2)}) collective-permute-start(bf16[272,128]{1,0:T(8,128)(2,1)S(1)} %get-tuple-element.22), channel_id=1, source_target_pairs={{0,2},{2,0},{4,6},{6,4},{8,10},{10,8},{12,14},{14,12},{1,3},{3,1},... | collective-permute-start | bytes 208904 | tf_op jit(solution)/shard_map/ppermute | solution.py:593

commit v4 on v3

--- a/solution.py
+++ b/solution.py
@@ -253,7 +253,7 @@
     quarter = chan_len // 4
     folded = jnp.abs(turn - 2 * quarter)
     angle = (folded - quarter).astype(jnp.float32) * (1.0 / quarter)
-    rotation = sine_quarter(angle).astype(jnp.bfloat16).astype(jnp.float32)
+    rotation = sine_quarter(angle).astype(jnp.bfloat16)
 
     flat = jnp.concatenate(
         [jnp.broadcast_to(taps_ref[tap : tap + 1, :], (8, chan_len)) for tap in range(plan.taps)]
@@ -269,39 +269,41 @@
     acc = jnp.zeros((count, columns), jnp.float32)
     order = sorted(range(plan.depth // LANES), key=lambda index: (index % blocks, index // blocks))
     turns = chan_len // LANES
-    batch = -(-blocks // 3)
-    arrived = 0
-    for piece in range(0, len(order), turns):
-        group = order[piece : piece + turns]
-        needed = max(index % blocks for index in group) // batch * batch + batch
-        while arrived < min(blocks, needed):
-            copies[arrived].wait()
-            arrived += 1
-        right = jnp.concatenate(
+    bounds = (9, blocks)
+
+    def column_tile(index):
+        scale = jnp.concatenate(
             [
-                (
-                    jnp.concatenate(
-                        [
-                            jnp.broadcast_to(
-                                taps_rows[shift_index, :, pl.ds(index * LANES, LANES)][None],
-                                (live // 8, 8, LANES),
-                            ).reshape(live, LANES)
-                            for shift_index in range(ROWS)
-                        ]
-                        * 2,
-                        axis=0,
-                    )
-                    * rotation[:, index % turns * LANES : (index % turns + 1) * LANES]
-                ).astype(jnp.bfloat16)
-                for index in group
+                jnp.broadcast_to(
+                    taps_rows[shift_index, :, pl.ds(index * LANES, LANES)][None],
+                    (live // 8, 8, LANES),
+                ).reshape(live, LANES)
+                for shift_index in range(ROWS)
             ],
-            axis=1,
-        )
-        left = jnp.concatenate(
-            [pairs[index % blocks, pl.ds(2 * (index // blocks), count), :] for index in group],
-            axis=1,
-        )
-        acc = acc + lax.dot_general(left, right, NT, preferred_element_type=jnp.float32)
+            axis=0,
+        ).astype(jnp.bfloat16)
+        turned = rotation[:, index % turns * LANES : (index % turns + 1) * LANES]
+        return jnp.concatenate([scale * turned[:half], scale * turned[half:]], axis=0)
+
+    groups = [order[piece : piece + turns] for piece in range(0, len(order), turns)]
+    (begin, seen) = (0, 0)
+    for bound in bounds:
+        end = begin
+        while end < len(groups) and max(index % blocks for index in groups[end]) < bound:
+            end += 1
+        staged = groups[begin:end]
+        rights = [
+            jnp.concatenate([column_tile(index) for index in group], axis=1) for group in staged
+        ]
+        for copy in copies[seen:bound]:
+            copy.wait()
+        for group, right in zip(staged, rights):
+            left = jnp.concatenate(
+                [pairs[index % blocks, pl.ds(2 * (index // blocks), count), :] for index in group],
+                axis=1,
+            )
+            acc = acc + lax.dot_general(left, right, NT, preferred_element_type=jnp.float32)
+        (begin, seen) = (end, bound)
     for tile in range(columns // LANES):
         total[tile] = acc[:, tile * LANES : (tile + 1) * LANES]
     (real_rows, imag_rows) = (
@@ -323,6 +325,7 @@
     code = ident * SLOT_LANES + imag * ROWS + shift
     out_lane = lax.broadcasted_iota(jnp.int32, (1, LANES), 1)
     slot = out_lane // SLOT_LANES
+    picks = []
     for step in range(plan.devices):
         target = jnp.bitwise_xor(tm * plan.zooms + zoom, step)
         (target_tm, target_zoom) = (target // plan.zooms, target % plan.zooms)
@@ -335,9 +338,16 @@
         valid = (position >= 0) & (position < width) & (slot < CH_DEV + 2)
         wanted = jnp.where(valid, (band_first + base) * SLOT_LANES + out_lane, -1)
         pick = (code == wanted).astype(jnp.float32).astype(jnp.bfloat16)
-        outs[step][...] = lax.dot_general(
-            coarse, pick, (((1,), (0,)), ((), ())), preferred_element_type=jnp.float32
-        ).astype(jnp.bfloat16)
+        picks.append(pick)
+
+    chosen = lax.dot_general(
+        coarse,
+        jnp.concatenate(picks, axis=1),
+        (((1,), (0,)), ((), ())),
+        preferred_element_type=jnp.float32,
+    ).astype(jnp.bfloat16)
+    for step in range(plan.devices):
+        outs[step][...] = chosen[:, step * LANES : (step + 1) * LANES]
 
 
 def fine_taps_kernel(plan, taps_ref, after_ref, out_ref):

time: 29.2 us -> 28.2 us (0.966)
  Pallas kernels: 11.7 us -> 10.7 us
    pallas_call x1, Pallas kernels: 9.17 us -> 8.2 us  [direct_plan(): pl.pallas_call(functools.partial(section_one_kernel, plan), out_shape=[bl...]
where the time goes in v4:
time: 28.2 us; the launch traced here: 27.9 us
  starting transfers between devices  13.9 us (49%)
  Pallas kernels  10.7 us (38%)
  waiting for transfers between devices  3.17 us (11%)
    ppermute x7, starting transfers between devices, direct_plan(): received[step] = lax.ppermute(sent[step], ('tm', 'zoom'), pairs)  13.9 us
    pallas_call x1, Pallas kernels, direct_plan(): pl.pallas_call(functools.partial(section_one_kernel, plan), out_shape=[bl...  8.2 us
    ppermute x7, waiting for transfers between devices, direct_plan(): received[step] = lax.ppermute(sent[step], ('tm', 'zoom'), pairs)  3.17 us
    pallas_call x1, Pallas kernels, direct_plan(): pl.pallas_call(functools.partial(section_two_kernel, plan, late), out_sha...  1.93 us
  transfers between devices with their start and end apart: 7, of which 3 were waited for; matrix products, arithmetic and copies ran while one was open for 0% of the time, Pallas kernels for 2%

profile of v4, /device:TPU:0, one launch (start us, length us, event | category | flops | bytes accessed | tf_op | source)
XLA Modules:
  0.0 27.9 jit_solution(409005839686760452)
XLA Ops:
  0.0 0.0 copy-start.3
  0.0 8.2 %section_one.1 = (bf16[272,128]{1,0:T(8,128)(2,1)S(1)}, bf16[272,128]{1,0:T(8,128)(2,1)S(1)}, bf16[272,128]{1,0:T(8,128)(2,1)S(1)}, bf16[272,128]{1,0:T(8,128)(2...) custom-call(s32[2]{0:T(128)} %starts_hbm.1, ...), custom_call_target="tpu_custom_call" | custom-call | tf_op jit(solution)/shard_map/section_one/pallas_call | solution.py:581
  8.2 5.1 %collective-permute-start = (bf16[272,128]{1,0:T(8,128)(2,1)S(1)}, bf16[272,128]{1,0:T(8,128)(2,1)S(1)}, u32[]{:S(2)}, u32[]{:S(2)}) collective-permute-start(bf16[272,128]{1,0:T(8,128)(2,1)S(1)} %get-tuple-element.15), channel_id=1, source_target_pairs={{0,12},{2,14},{4,8},{6,10},{8,4},{10,6},{12,0},{14,2},{1,13},{3,15... | collective-permute-start | bytes 208904 | tf_op jit(solution)/shard_map/ppermute | solution.py:603
  13.4 1.1 %collective-permute-start.1 = (bf16[272,128]{1,0:T(8,128)(2,1)S(1)}, bf16[272,128]{1,0:T(8,128)(2,1)S(1)}, u32[]{:S(2)}, u32[]{:S(2)}) collective-permute-start(bf16[272,128]{1,0:T(8,128)(2,1)S(1)} %get-tuple-element.17), channel_id=1, source_target_pairs={{0,14},{2,12},{4,10},{6,8},{8,6},{10,4},{12,2},{14,0},{1,15},{3,13... | collective-permute-start | bytes 208904 | tf_op jit(solution)/shard_map/ppermute | solution.py:603
  14.5 0.8 %collective-permute-start.2 = (bf16[272,128]{1,0:T(8,128)(2,1)S(1)}, bf16[272,128]{1,0:T(8,128)(2,1)S(1)}, u32[]{:S(2)}, u32[]{:S(2)}) collective-permute-start(bf16[272,128]{1,0:T(8,128)(2,1)S(1)} %get-tuple-element.18), channel_id=1, source_target_pairs={{0,10},{2,8},{4,14},{6,12},{8,2},{10,0},{12,6},{14,4},{1,11},{3,9}... | collective-permute-start | bytes 208904 | tf_op jit(solution)/shard_map/ppermute | solution.py:603
  15.3 2.0 %collective-permute-start.3 = (bf16[272,128]{1,0:T(8,128)(2,1)S(1)}, bf16[272,128]{1,0:T(8,128)(2,1)S(1)}, u32[]{:S(2)}, u32[]{:S(2)}) collective-permute-start(bf16[272,128]{1,0:T(8,128)(2,1)S(1)} %get-tuple-element.19), channel_id=1, source_target_pairs={{0,8},{2,10},{4,12},{6,14},{8,0},{10,2},{12,4},{14,6},{1,9},{3,11}... | collective-permute-start | bytes 208904 | tf_op jit(solution)/shard_map/ppermute | solution.py:603
  17.3 2.3 %collective-permute-start.4 = (bf16[272,128]{1,0:T(8,128)(2,1)S(1)}, bf16[272,128]{1,0:T(8,128)(2,1)S(1)}, u32[]{:S(2)}, u32[]{:S(2)}) collective-permute-start(bf16[272,128]{1,0:T(8,128)(2,1)S(1)} %get-tuple-element.20), channel_id=1, source_target_pairs={{0,6},{2,4},{4,2},{6,0},{8,14},{10,12},{12,10},{14,8},{1,7},{3,5},... | collective-permute-start | bytes 208904 | tf_op jit(solution)/shard_map/ppermute | solution.py:603
  19.6 0.0 collective-permute-done.after_ref.rest_2_
  19.6 1.3 %collective-permute-start.5 = (bf16[272,128]{1,0:T(8,128)(2,1)S(1)}, bf16[272,128]{1,0:T(8,128)(2,1)S(1)}, u32[]{:S(2)}, u32[]{:S(2)}) collective-permute-start(bf16[272,128]{1,0:T(8,128)(2,1)S(1)} %get-tuple-element.21), channel_id=1, source_target_pairs={{0,4},{2,6},{4,0},{6,2},{8,12},{10,14},{12,8},{14,10},{1,5},{3,7},... | collective-permute-start | bytes 208904 | tf_op jit(solution)/shard_map/ppermute | solution.py:603
  20.9 0.0 collective-permute-done.1.rest_1_
  20.9 1.2 %collective-permute-start.6 = (bf16[272,128]{1,0:T(8,128)(2,1)S(1)}, bf16[272,128]{1,0:T(8,128)(2,1)S(1)}, u32[]{:S(2)}, u32[]{:S(2)}) collective-permute-start(bf16[272,128]{1,0:T(8,128)(2,1)S(1)} %get-tuple-element.22), channel_id=1, source_target_pairs={{0,2},{2,0},{4,6},{6,4},{8,10},{10,8},{12,14},{14,12},{1,3},{3,1},... | collective-permute-start | bytes 208904 | tf_op jit(solution)/shard_map/ppermute | solution.py:603
  22.1 0.0 copy-done.4
  22.1 0.5 %fine_taps.1.taps_ref = f32[2168,128]{1,0:T(8,128)S(1)} custom-call(f32[5,3456]{1,0:T(8,128)S(1)} %copy-done.4, bf16[272,128]{1,0:T(8,128)(2,1)S(1)} %collective-permute-done.after_ref.rest_2_), custom_call_target="tpu_custom_call" | custom-call | tf_op jit(solution)/shard_map/fine_taps/pallas_call | solution.py:607
  22.6 2.5 %collective-permute-done.2.rest_3_ = bf16[272,128]{1,0:T(8,128)(2,1)S(1)} collective-permute-done((bf16[272,128]{1,0:T(8,128)(2,1)S(1)}, bf16[272,128]{1,0:T(8,128)(2,1)S(1)}, u32[]{:S(2)}, u32[]{:S(2)}) %collective-permute-start.2) | collective-permute-done | bytes 69664 | tf_op jit(solution)/shard_map/ppermute | solution.py:603
  25.1 0.2 collective-permute-done.3.rest_4_
  25.3 0.1 merge.1.kept_ref
  25.4 0.0 collective-permute-done.4.rest_0_
  25.5 0.5 %collective-permute-done.5.rest_1_ = bf16[272,128]{1,0:T(8,128)(2,1)S(1)} collective-permute-done((bf16[272,128]{1,0:T(8,128)(2,1)S(1)}, bf16[272,128]{1,0:T(8,128)(2,1)S(1)}, u32[]{:S(2)}, u32[]{:S(2)}) %collective-permute-start.5) | collective-permute-done | bytes 69664 | tf_op jit(solution)/shard_map/ppermute | solution.py:603
  25.9 0.0 collective-permute-done.6.rest_2_
  25.9 0.0 copy-done.3
  25.9 0.0 copy-done.1
  25.9 0.0 copy-done.2
  25.9 0.0 copy-done
  25.9 1.9 %section_two.1 = f32[2,1,14580]{2,1,0:T(1,128)} custom-call(s32[8,128]{1,0:T(8,128)S(1)} %get-tuple-element.14.width_ref, f32[432,128]{1,0:T(8,128)S(1)} %merge.1.kept_ref, f32[2168,128]{1,0:T(8,128)S(1)} %fine_taps.1.taps_ref, bf16[1024,432]{1,0:T(8,128)(2,1)S(1)} %copy-done, f32[512,128]{1,0:T(8,128)S(1)} %copy-done.2, f32[512,128]{1,0:T(8,128)S(1)} %copy-done.1, ...), custom_call_target="tpu_custom_call" | custom-call | tf_op jit(solution)/shard_map/section_two/pallas_call | solution.py:626
  (4 shorter events, 0.0 us)
Async XLA Ops:
  0.0 25.9 %copy-start.3 = (bf16[128,512]{1,0:T(8,128)(2,1)S(1)}, bf16[128,512]{1,0:T(8,128)(2,1)}, u32[]{:S(2)}) copy-start(bf16[128,512]{1,0:T(8,128)(2,1)} %constant.11.clone.join_ref) | copy-start | bytes 393220
  0.0 25.9 %copy-start.1 = (f32[512,128]{1,0:T(8,128)S(1)}, f32[512,128]{1,0:T(8,128)}, u32[]{:S(2)}) copy-start(f32[512,128]{1,0:T(8,128)} %constant.10.clone.sin_ref) | copy-start | bytes 786436
  0.0 25.9 %copy-start.2 = (f32[512,128]{1,0:T(8,128)S(1)}, f32[512,128]{1,0:T(8,128)}, u32[]{:S(2)}) copy-start(f32[512,128]{1,0:T(8,128)} %constant.9.clone.cos_ref) | copy-start | bytes 786436
  0.0 25.9 %copy-start = (bf16[1024,432]{1,0:T(8,128)(2,1)S(1)}, bf16[1024,432]{1,0:T(8,128)(2,1)}, u32[]{:S(2)}) copy-start(bf16[1024,432]{1,0:T(8,128)(2,1)} %constant.8.clone.dft_ref) | copy-start | bytes 2654212
  0.0 22.1 %copy-start.4 = (f32[5,3456]{1,0:T(8,128)S(1)}, f32[5,3456]{1,0:T(8,128)}, u32[]{:S(2)}) copy-start(f32[5,3456]{1,0:T(8,128)} %taps_ref.1) | copy-start | bytes 207364
  8.2 11.4 %collective-permute-start = (bf16[272,128]{1,0:T(8,128)(2,1)S(1)}, bf16[272,128]{1,0:T(8,128)(2,1)S(1)}, u32[]{:S(2)}, u32[]{:S(2)}) collective-permute-start(bf16[272,128]{1,0:T(8,128)(2,1)S(1)} %get-tuple-element.15), channel_id=1, source_target_pairs={{0,12},{2,14},{4,8},{6,10},{8,4},{10,6},{12,0},{14,2},{1,13},{3,15... | collective-permute-start | bytes 208904 | tf_op jit(solution)/shard_map/ppermute | solution.py:603
  13.4 7.5 %collective-permute-start.1 = (bf16[272,128]{1,0:T(8,128)(2,1)S(1)}, bf16[272,128]{1,0:T(8,128)(2,1)S(1)}, u32[]{:S(2)}, u32[]{:S(2)}) collective-permute-start(bf16[272,128]{1,0:T(8,128)(2,1)S(1)} %get-tuple-element.17), channel_id=1, source_target_pairs={{0,14},{2,12},{4,10},{6,8},{8,6},{10,4},{12,2},{14,0},{1,15},{3,13... | collective-permute-start | bytes 208904 | tf_op jit(solution)/shard_map/ppermute | solution.py:603
  14.5 10.6 %collective-permute-start.2 = (bf16[272,128]{1,0:T(8,128)(2,1)S(1)}, bf16[272,128]{1,0:T(8,128)(2,1)S(1)}, u32[]{:S(2)}, u32[]{:S(2)}) collective-permute-start(bf16[272,128]{1,0:T(8,128)(2,1)S(1)} %get-tuple-element.18), channel_id=1, source_target_pairs={{0,10},{2,8},{4,14},{6,12},{8,2},{10,0},{12,6},{14,4},{1,11},{3,9}... | collective-permute-start | bytes 208904 | tf_op jit(solution)/shard_map/ppermute | solution.py:603
  15.3 10.0 %collective-permute-start.3 = (bf16[272,128]{1,0:T(8,128)(2,1)S(1)}, bf16[272,128]{1,0:T(8,128)(2,1)S(1)}, u32[]{:S(2)}, u32[]{:S(2)}) collective-permute-start(bf16[272,128]{1,0:T(8,128)(2,1)S(1)} %get-tuple-element.19), channel_id=1, source_target_pairs={{0,8},{2,10},{4,12},{6,14},{8,0},{10,2},{12,4},{14,6},{1,9},{3,11}... | collective-permute-start | bytes 208904 | tf_op jit(solution)/shard_map/ppermute | solution.py:603
  17.3 8.2 %collective-permute-start.4 = (bf16[272,128]{1,0:T(8,128)(2,1)S(1)}, bf16[272,128]{1,0:T(8,128)(2,1)S(1)}, u32[]{:S(2)}, u32[]{:S(2)}) collective-permute-start(bf16[272,128]{1,0:T(8,128)(2,1)S(1)} %get-tuple-element.20), channel_id=1, source_target_pairs={{0,6},{2,4},{4,2},{6,0},{8,14},{10,12},{12,10},{14,8},{1,7},{3,5},... | collective-permute-start | bytes 208904 | tf_op jit(solution)/shard_map/ppermute | solution.py:603
  19.6 6.3 %collective-permute-start.5 = (bf16[272,128]{1,0:T(8,128)(2,1)S(1)}, bf16[272,128]{1,0:T(8,128)(2,1)S(1)}, u32[]{:S(2)}, u32[]{:S(2)}) collective-permute-start(bf16[272,128]{1,0:T(8,128)(2,1)S(1)} %get-tuple-element.21), channel_id=1, source_target_pairs={{0,4},{2,6},{4,0},{6,2},{8,12},{10,14},{12,8},{14,10},{1,5},{3,7},... | collective-permute-start | bytes 208904 | tf_op jit(solution)/shard_map/ppermute | solution.py:603
  20.9 5.0 %collective-permute-start.6 = (bf16[272,128]{1,0:T(8,128)(2,1)S(1)}, bf16[272,128]{1,0:T(8,128)(2,1)S(1)}, u32[]{:S(2)}, u32[]{:S(2)}) collective-permute-start(bf16[272,128]{1,0:T(8,128)(2,1)S(1)} %get-tuple-element.22), channel_id=1, source_target_pairs={{0,2},{2,0},{4,6},{6,4},{8,10},{10,8},{12,14},{14,12},{1,3},{3,1},... | collective-permute-start | bytes 208904 | tf_op jit(solution)/shard_map/ppermute | solution.py:603

commit v5 on v4

--- a/solution.py
+++ b/solution.py
@@ -403,8 +403,8 @@
     (fine_rows, bins) = (plan.fine_rows, plan.bins)
     fine_in = kept_ref[...] + add_blocks(plan, steps, taps_ref, blocks, sums)
     spun = lax.dot_general(
+        fine_in.T.astype(jnp.bfloat16),
         dft_ref[...],
-        fine_in.astype(jnp.bfloat16),
         (((1,), (0,)), ((), ())),
         preferred_element_type=jnp.float32,
     )
@@ -412,12 +412,14 @@
     mixed = jnp.concatenate(
         [
             (part * factor).astype(jnp.bfloat16)
-            for part in (spun[:bins], spun[bins:])
+            for part in (spun[:, :bins], spun[:, bins:])
             for factor in (cosine_tab, sine_tab)
         ],
-        axis=1,
-    )
-    joined = lax.dot_general(join_ref[...], mixed, NT, preferred_element_type=jnp.float32)
+        axis=0,
+    )
+    joined = lax.dot_general(
+        join_ref[...], mixed, (((1,), (0,)), ((), ())), preferred_element_type=jnp.float32
+    )
 
     slots = LANES // SLOT_LANES
     high = 2 * slots
@@ -519,9 +521,9 @@
         imag[:, 2, 0], imag[:, 2, 1] = (-cosine, -sine)
         imag[:, 3, 0], imag[:, 3, 1] = (sine, -cosine)
     return (
-        jnp.asarray(dft, jnp.bfloat16),
-        jnp.asarray(np.pad(np.cos(twist), margin), jnp.float32),
-        jnp.asarray(np.pad(np.sin(twist), margin), jnp.float32),
+        jnp.asarray(dft.T, jnp.bfloat16),
+        jnp.asarray(np.pad(np.cos(twist), margin).T, jnp.float32),
+        jnp.asarray(np.pad(np.sin(twist), margin).T, jnp.float32),
         jnp.asarray(join.reshape(LANES, 4 * LANES), jnp.bfloat16),
     )
 

time: 28.2 us -> 28 us (level)
  Pallas kernels: 10.7 us -> 10.4 us
where the time goes in v5:
time: 28 us; the launch traced here: 27.6 us
  starting transfers between devices  13.9 us (50%)
  Pallas kernels  10.4 us (37%)
  waiting for transfers between devices  3.17 us (11%)
    ppermute x7, starting transfers between devices, direct_plan(): received[step] = lax.ppermute(sent[step], ('tm', 'zoom'), pairs)  13.9 us
    pallas_call x1, Pallas kernels, direct_plan(): pl.pallas_call(functools.partial(section_one_kernel, plan), out_shape=[bl...  8.2 us
    ppermute x7, waiting for transfers between devices, direct_plan(): received[step] = lax.ppermute(sent[step], ('tm', 'zoom'), pairs)  3.17 us
    pallas_call x1, Pallas kernels, direct_plan(): pl.pallas_call(functools.partial(section_two_kernel, plan, late), out_sha...  1.65 us
  transfers between devices with their start and end apart: 7, of which 3 were waited for; matrix products, arithmetic and copies ran while one was open for 0% of the time, Pallas kernels for 2%

profile of v5, /device:TPU:0, one launch (start us, length us, event | category | flops | bytes accessed | tf_op | source)
XLA Modules:
  0.0 27.6 jit_solution(13820953498878254839)
XLA Ops:
  0.0 0.0 copy-start.3
  0.0 8.2 %section_one.1 = (bf16[272,128]{1,0:T(8,128)(2,1)S(1)}, bf16[272,128]{1,0:T(8,128)(2,1)S(1)}, bf16[272,128]{1,0:T(8,128)(2,1)S(1)}, bf16[272,128]{1,0:T(8,128)(2...) custom-call(s32[2]{0:T(128)} %starts_hbm.1, ...), custom_call_target="tpu_custom_call" | custom-call | tf_op jit(solution)/shard_map/section_one/pallas_call | solution.py:583
  8.2 5.1 %collective-permute-start = (bf16[272,128]{1,0:T(8,128)(2,1)S(1)}, bf16[272,128]{1,0:T(8,128)(2,1)S(1)}, u32[]{:S(2)}, u32[]{:S(2)}) collective-permute-start(bf16[272,128]{1,0:T(8,128)(2,1)S(1)} %get-tuple-element.15), channel_id=1, source_target_pairs={{0,12},{2,14},{4,8},{6,10},{8,4},{10,6},{12,0},{14,2},{1,13},{3,15... | collective-permute-start | bytes 208904 | tf_op jit(solution)/shard_map/ppermute | solution.py:605
  13.4 1.1 %collective-permute-start.1 = (bf16[272,128]{1,0:T(8,128)(2,1)S(1)}, bf16[272,128]{1,0:T(8,128)(2,1)S(1)}, u32[]{:S(2)}, u32[]{:S(2)}) collective-permute-start(bf16[272,128]{1,0:T(8,128)(2,1)S(1)} %get-tuple-element.17), channel_id=1, source_target_pairs={{0,14},{2,12},{4,10},{6,8},{8,6},{10,4},{12,2},{14,0},{1,15},{3,13... | collective-permute-start | bytes 208904 | tf_op jit(solution)/shard_map/ppermute | solution.py:605
  14.5 0.8 %collective-permute-start.2 = (bf16[272,128]{1,0:T(8,128)(2,1)S(1)}, bf16[272,128]{1,0:T(8,128)(2,1)S(1)}, u32[]{:S(2)}, u32[]{:S(2)}) collective-permute-start(bf16[272,128]{1,0:T(8,128)(2,1)S(1)} %get-tuple-element.18), channel_id=1, source_target_pairs={{0,10},{2,8},{4,14},{6,12},{8,2},{10,0},{12,6},{14,4},{1,11},{3,9}... | collective-permute-start | bytes 208904 | tf_op jit(solution)/shard_map/ppermute | solution.py:605
  15.3 2.0 %collective-permute-start.3 = (bf16[272,128]{1,0:T(8,128)(2,1)S(1)}, bf16[272,128]{1,0:T(8,128)(2,1)S(1)}, u32[]{:S(2)}, u32[]{:S(2)}) collective-permute-start(bf16[272,128]{1,0:T(8,128)(2,1)S(1)} %get-tuple-element.19), channel_id=1, source_target_pairs={{0,8},{2,10},{4,12},{6,14},{8,0},{10,2},{12,4},{14,6},{1,9},{3,11}... | collective-permute-start | bytes 208904 | tf_op jit(solution)/shard_map/ppermute | solution.py:605
  17.3 2.3 %collective-permute-start.4 = (bf16[272,128]{1,0:T(8,128)(2,1)S(1)}, bf16[272,128]{1,0:T(8,128)(2,1)S(1)}, u32[]{:S(2)}, u32[]{:S(2)}) collective-permute-start(bf16[272,128]{1,0:T(8,128)(2,1)S(1)} %get-tuple-element.20), channel_id=1, source_target_pairs={{0,6},{2,4},{4,2},{6,0},{8,14},{10,12},{12,10},{14,8},{1,7},{3,5},... | collective-permute-start | bytes 208904 | tf_op jit(solution)/shard_map/ppermute | solution.py:605
  19.6 0.0 collective-permute-done.after_ref.rest_2_
  19.6 1.3 %collective-permute-start.5 = (bf16[272,128]{1,0:T(8,128)(2,1)S(1)}, bf16[272,128]{1,0:T(8,128)(2,1)S(1)}, u32[]{:S(2)}, u32[]{:S(2)}) collective-permute-start(bf16[272,128]{1,0:T(8,128)(2,1)S(1)} %get-tuple-element.21), channel_id=1, source_target_pairs={{0,4},{2,6},{4,0},{6,2},{8,12},{10,14},{12,8},{14,10},{1,5},{3,7},... | collective-permute-start | bytes 208904 | tf_op jit(solution)/shard_map/ppermute | solution.py:605
  20.9 0.0 collective-permute-done.1.rest_1_
  20.9 1.2 %collective-permute-start.6 = (bf16[272,128]{1,0:T(8,128)(2,1)S(1)}, bf16[272,128]{1,0:T(8,128)(2,1)S(1)}, u32[]{:S(2)}, u32[]{:S(2)}) collective-permute-start(bf16[272,128]{1,0:T(8,128)(2,1)S(1)} %get-tuple-element.22), channel_id=1, source_target_pairs={{0,2},{2,0},{4,6},{6,4},{8,10},{10,8},{12,14},{14,12},{1,3},{3,1},... | collective-permute-start | bytes 208904 | tf_op jit(solution)/shard_map/ppermute | solution.py:605
  22.1 0.0 copy-done.4
  22.1 0.5 %fine_taps.1.taps_ref = f32[2168,128]{1,0:T(8,128)S(1)} custom-call(f32[5,3456]{1,0:T(8,128)S(1)} %copy-done.4, bf16[272,128]{1,0:T(8,128)(2,1)S(1)} %collective-permute-done.after_ref.rest_2_), custom_call_target="tpu_custom_call" | custom-call | tf_op jit(solution)/shard_map/fine_taps/pallas_call | solution.py:609
  22.6 2.5 %collective-permute-done.2.rest_3_ = bf16[272,128]{1,0:T(8,128)(2,1)S(1)} collective-permute-done((bf16[272,128]{1,0:T(8,128)(2,1)S(1)}, bf16[272,128]{1,0:T(8,128)(2,1)S(1)}, u32[]{:S(2)}, u32[]{:S(2)}) %collective-permute-start.2) | collective-permute-done | bytes 69664 | tf_op jit(solution)/shard_map/ppermute | solution.py:605
  25.1 0.2 collective-permute-done.3.rest_4_
  25.3 0.1 merge.1.kept_ref
  25.4 0.0 collective-permute-done.4.rest_0_
  25.5 0.5 %collective-permute-done.5.rest_1_ = bf16[272,128]{1,0:T(8,128)(2,1)S(1)} collective-permute-done((bf16[272,128]{1,0:T(8,128)(2,1)S(1)}, bf16[272,128]{1,0:T(8,128)(2,1)S(1)}, u32[]{:S(2)}, u32[]{:S(2)}) %collective-permute-start.5) | collective-permute-done | bytes 69664 | tf_op jit(solution)/shard_map/ppermute | solution.py:605
  25.9 0.0 collective-permute-done.6.rest_2_
  25.9 0.0 copy-done.3
  25.9 0.0 copy-done.1
  25.9 0.0 copy-done.2
  25.9 0.0 copy-done
  25.9 1.6 %section_two.1 = f32[2,1,14580]{2,1,0:T(1,128)} custom-call(s32[8,128]{1,0:T(8,128)S(1)} %get-tuple-element.14.width_ref, f32[432,128]{1,0:T(8,128)S(1)} %merge.1.kept_ref, f32[2168,128]{1,0:T(8,128)S(1)} %fine_taps.1.taps_ref, bf16[432,1024]{1,0:T(8,128)(2,1)S(1)} %copy-done, f32[128,512]{1,0:T(8,128)S(1)} %copy-done.2, f32[128,512]{1,0:T(8,128)S(1)} %copy-done.1, ...), custom_call_target="tpu_custom_call" | custom-call | tf_op jit(solution)/shard_map/section_two/pallas_call | solution.py:628
  (4 shorter events, 0.0 us)
Async XLA Ops:
  0.0 25.9 %copy-start.3 = (bf16[128,512]{1,0:T(8,128)(2,1)S(1)}, bf16[128,512]{1,0:T(8,128)(2,1)}, u32[]{:S(2)}) copy-start(bf16[128,512]{1,0:T(8,128)(2,1)} %constant.11.clone.join_ref) | copy-start | bytes 393220
  0.0 25.9 %copy-start.1 = (f32[128,512]{1,0:T(8,128)S(1)}, f32[128,512]{1,0:T(8,128)}, u32[]{:S(2)}) copy-start(f32[128,512]{1,0:T(8,128)} %constant.10.clone.sin_ref) | copy-start | bytes 786436
  0.0 25.9 %copy-start.2 = (f32[128,512]{1,0:T(8,128)S(1)}, f32[128,512]{1,0:T(8,128)}, u32[]{:S(2)}) copy-start(f32[128,512]{1,0:T(8,128)} %constant.9.clone.cos_ref) | copy-start | bytes 786436
  0.0 25.9 %copy-start = (bf16[432,1024]{1,0:T(8,128)(2,1)S(1)}, bf16[432,1024]{1,0:T(8,128)(2,1)}, u32[]{:S(2)}) copy-start(bf16[432,1024]{1,0:T(8,128)(2,1)} %constant.8.clone.dft_ref) | copy-start | bytes 2654212
  0.0 22.1 %copy-start.4 = (f32[5,3456]{1,0:T(8,128)S(1)}, f32[5,3456]{1,0:T(8,128)}, u32[]{:S(2)}) copy-start(f32[5,3456]{1,0:T(8,128)} %taps_ref.1) | copy-start | bytes 207364
  8.2 11.4 %collective-permute-start = (bf16[272,128]{1,0:T(8,128)(2,1)S(1)}, bf16[272,128]{1,0:T(8,128)(2,1)S(1)}, u32[]{:S(2)}, u32[]{:S(2)}) collective-permute-start(bf16[272,128]{1,0:T(8,128)(2,1)S(1)} %get-tuple-element.15), channel_id=1, source_target_pairs={{0,12},{2,14},{4,8},{6,10},{8,4},{10,6},{12,0},{14,2},{1,13},{3,15... | collective-permute-start | bytes 208904 | tf_op jit(solution)/shard_map/ppermute | solution.py:605
  13.4 7.5 %collective-permute-start.1 = (bf16[272,128]{1,0:T(8,128)(2,1)S(1)}, bf16[272,128]{1,0:T(8,128)(2,1)S(1)}, u32[]{:S(2)}, u32[]{:S(2)}) collective-permute-start(bf16[272,128]{1,0:T(8,128)(2,1)S(1)} %get-tuple-element.17), channel_id=1, source_target_pairs={{0,14},{2,12},{4,10},{6,8},{8,6},{10,4},{12,2},{14,0},{1,15},{3,13... | collective-permute-start | bytes 208904 | tf_op jit(solution)/shard_map/ppermute | solution.py:605
  14.5 10.6 %collective-permute-start.2 = (bf16[272,128]{1,0:T(8,128)(2,1)S(1)}, bf16[272,128]{1,0:T(8,128)(2,1)S(1)}, u32[]{:S(2)}, u32[]{:S(2)}) collective-permute-start(bf16[272,128]{1,0:T(8,128)(2,1)S(1)} %get-tuple-element.18), channel_id=1, source_target_pairs={{0,10},{2,8},{4,14},{6,12},{8,2},{10,0},{12,6},{14,4},{1,11},{3,9}... | collective-permute-start | bytes 208904 | tf_op jit(solution)/shard_map/ppermute | solution.py:605
  15.3 10.0 %collective-permute-start.3 = (bf16[272,128]{1,0:T(8,128)(2,1)S(1)}, bf16[272,128]{1,0:T(8,128)(2,1)S(1)}, u32[]{:S(2)}, u32[]{:S(2)}) collective-permute-start(bf16[272,128]{1,0:T(8,128)(2,1)S(1)} %get-tuple-element.19), channel_id=1, source_target_pairs={{0,8},{2,10},{4,12},{6,14},{8,0},{10,2},{12,4},{14,6},{1,9},{3,11}... | collective-permute-start | bytes 208904 | tf_op jit(solution)/shard_map/ppermute | solution.py:605
  17.3 8.2 %collective-permute-start.4 = (bf16[272,128]{1,0:T(8,128)(2,1)S(1)}, bf16[272,128]{1,0:T(8,128)(2,1)S(1)}, u32[]{:S(2)}, u32[]{:S(2)}) collective-permute-start(bf16[272,128]{1,0:T(8,128)(2,1)S(1)} %get-tuple-element.20), channel_id=1, source_target_pairs={{0,6},{2,4},{4,2},{6,0},{8,14},{10,12},{12,10},{14,8},{1,7},{3,5},... | collective-permute-start | bytes 208904 | tf_op jit(solution)/shard_map/ppermute | solution.py:605
  19.6 6.3 %collective-permute-start.5 = (bf16[272,128]{1,0:T(8,128)(2,1)S(1)}, bf16[272,128]{1,0:T(8,128)(2,1)S(1)}, u32[]{:S(2)}, u32[]{:S(2)}) collective-permute-start(bf16[272,128]{1,0:T(8,128)(2,1)S(1)} %get-tuple-element.21), channel_id=1, source_target_pairs={{0,4},{2,6},{4,0},{6,2},{8,12},{10,14},{12,8},{14,10},{1,5},{3,7},... | collective-permute-start | bytes 208904 | tf_op jit(solution)/shard_map/ppermute | solution.py:605
  20.9 5.0 %collective-permute-start.6 = (bf16[272,128]{1,0:T(8,128)(2,1)S(1)}, bf16[272,128]{1,0:T(8,128)(2,1)S(1)}, u32[]{:S(2)}, u32[]{:S(2)}) collective-permute-start(bf16[272,128]{1,0:T(8,128)(2,1)S(1)} %get-tuple-element.22), channel_id=1, source_target_pairs={{0,2},{2,0},{4,6},{6,4},{8,10},{10,8},{12,14},{14,12},{1,3},{3,1},... | collective-permute-start | bytes 208904 | tf_op jit(solution)/shard_map/ppermute | solution.py:605

commit v6 on v5

--- a/solution.py
+++ b/solution.py
@@ -248,22 +248,37 @@
         channel = jnp.where(inside, starts_ref[band] + ident - first, channel)
         firsts.append(first)
         first = first + widths_ref[band]
-    phase = lax.broadcasted_iota(jnp.int32, (columns, chan_len), 1) - HOP * shift
-    turn = (channel * phase + imag * (chan_len // 4)) & (chan_len - 1)
+    phase = lax.broadcasted_iota(jnp.int32, (columns, LANES), 1) - HOP * shift
     quarter = chan_len // 4
+    turn = (channel * phase + imag * quarter) & (chan_len - 1)
     folded = jnp.abs(turn - 2 * quarter)
     angle = (folded - quarter).astype(jnp.float32) * (1.0 / quarter)
-    rotation = sine_quarter(angle).astype(jnp.bfloat16)
-
+    first_lanes = sine_quarter(angle)
+    ahead = jnp.concatenate([first_lanes[half:], -first_lanes[:half]], axis=0)
+    tiles = [first_lanes]
+    for tile in range(1, 4):
+        quarters = (channel * tile) & 3
+        same = (quarters == 0).astype(jnp.float32) - (quarters == 2).astype(jnp.float32)
+        next_one = (quarters == 1).astype(jnp.float32) - (quarters == 3).astype(jnp.float32)
+        tiles.append(same * first_lanes + next_one * ahead)
+    rotation = jnp.concatenate(tiles, axis=1).astype(jnp.bfloat16)
+
+    filled = plan.taps * chan_len + LANES
     flat = jnp.concatenate(
         [jnp.broadcast_to(taps_ref[tap : tap + 1, :], (8, chan_len)) for tap in range(plan.taps)]
-        + [jnp.zeros((8, plan.depth - plan.taps * chan_len), jnp.float32)],
+        + [jnp.zeros((8, LANES), jnp.float32)],
         axis=1,
     )
     for shift_index in range(ROWS):
-        taps_rows[shift_index] = (
-            pltpu.roll(flat, HOP * shift_index, axis=1) if shift_index else flat
-        )
+        (skipped, offset) = divmod(HOP * shift_index, LANES)
+        moved = pltpu.roll(flat, offset, axis=1) if offset else flat
+        first = skipped * LANES
+        end = min(first + filled, plan.depth)
+        if first:
+            taps_rows[shift_index, :, :first] = jnp.zeros((8, first), jnp.float32)
+        taps_rows[shift_index, :, first:end] = moved[:, : end - first]
+        if end < plan.depth:
+            taps_rows[shift_index, :, end:] = jnp.zeros((8, plan.depth - end), jnp.float32)
     count = 2 * plan.out_rows
     pairs = frames.reshape(blocks, 2 * (plan.local_rows + 2 * lead), LANES)
     acc = jnp.zeros((count, columns), jnp.float32)
@@ -553,7 +568,7 @@
             self.row_len % LANES == 0
             and self.samples % self.row_len == 0
             and self.chan_len & (self.chan_len - 1) == 0
-            and self.chan_len % LANES == 0
+            and self.chan_len == 4 * LANES
             and self.devices & (self.devices - 1) == 0
             and self.live % 8 == 0
             and (2 * ROWS * self.live) % LANES == 0

time: 28 us -> 27.8 us (level)
  no operation moved by 1% of the time
where the time goes in v6:
time: 27.8 us; the launch traced here: 27.4 us
  starting transfers between devices  13.9 us (50%)
  Pallas kernels  10.3 us (37%)
  waiting for transfers between devices  3.19 us (11%)
    ppermute x7, starting transfers between devices, direct_plan(): received[step] = lax.ppermute(sent[step], ('tm', 'zoom'), pairs)  13.9 us
    pallas_call x1, Pallas kernels, direct_plan(): pl.pallas_call(functools.partial(section_one_kernel, plan), out_shape=[bl...  8.04 us
    ppermute x7, waiting for transfers between devices, direct_plan(): received[step] = lax.ppermute(sent[step], ('tm', 'zoom'), pairs)  3.19 us
    pallas_call x1, Pallas kernels, direct_plan(): pl.pallas_call(functools.partial(section_two_kernel, plan, late), out_sha...  1.65 us
  transfers between devices with their start and end apart: 7, of which 3 were waited for; matrix products, arithmetic and copies ran while one was open for 0% of the time, Pallas kernels for 2%

profile of v6, /device:TPU:0, one launch (start us, length us, event | category | flops | bytes accessed | tf_op | source)
XLA Modules:
  0.0 27.4 jit_solution(15617952628994633264)
XLA Ops:
  0.0 0.0 copy-start.3
  0.0 8.0 %section_one.1 = (bf16[272,128]{1,0:T(8,128)(2,1)S(1)}, bf16[272,128]{1,0:T(8,128)(2,1)S(1)}, bf16[272,128]{1,0:T(8,128)(2,1)S(1)}, bf16[272,128]{1,0:T(8,128)(2...) custom-call(s32[2]{0:T(128)} %starts_hbm.1, ...), custom_call_target="tpu_custom_call" | custom-call | tf_op jit(solution)/shard_map/section_one/pallas_call | solution.py:598
  8.1 5.1 %collective-permute-start = (bf16[272,128]{1,0:T(8,128)(2,1)S(1)}, bf16[272,128]{1,0:T(8,128)(2,1)S(1)}, u32[]{:S(2)}, u32[]{:S(2)}) collective-permute-start(bf16[272,128]{1,0:T(8,128)(2,1)S(1)} %get-tuple-element.15), channel_id=1, source_target_pairs={{0,12},{2,14},{4,8},{6,10},{8,4},{10,6},{12,0},{14,2},{1,13},{3,15... | collective-permute-start | bytes 208904 | tf_op jit(solution)/shard_map/ppermute | solution.py:620
  13.2 1.2 %collective-permute-start.1 = (bf16[272,128]{1,0:T(8,128)(2,1)S(1)}, bf16[272,128]{1,0:T(8,128)(2,1)S(1)}, u32[]{:S(2)}, u32[]{:S(2)}) collective-permute-start(bf16[272,128]{1,0:T(8,128)(2,1)S(1)} %get-tuple-element.17), channel_id=1, source_target_pairs={{0,14},{2,12},{4,10},{6,8},{8,6},{10,4},{12,2},{14,0},{1,15},{3,13... | collective-permute-start | bytes 208904 | tf_op jit(solution)/shard_map/ppermute | solution.py:620
  14.3 0.8 %collective-permute-start.2 = (bf16[272,128]{1,0:T(8,128)(2,1)S(1)}, bf16[272,128]{1,0:T(8,128)(2,1)S(1)}, u32[]{:S(2)}, u32[]{:S(2)}) collective-permute-start(bf16[272,128]{1,0:T(8,128)(2,1)S(1)} %get-tuple-element.18), channel_id=1, source_target_pairs={{0,10},{2,8},{4,14},{6,12},{8,2},{10,0},{12,6},{14,4},{1,11},{3,9}... | collective-permute-start | bytes 208904 | tf_op jit(solution)/shard_map/ppermute | solution.py:620
  15.1 2.0 %collective-permute-start.3 = (bf16[272,128]{1,0:T(8,128)(2,1)S(1)}, bf16[272,128]{1,0:T(8,128)(2,1)S(1)}, u32[]{:S(2)}, u32[]{:S(2)}) collective-permute-start(bf16[272,128]{1,0:T(8,128)(2,1)S(1)} %get-tuple-element.19), channel_id=1, source_target_pairs={{0,8},{2,10},{4,12},{6,14},{8,0},{10,2},{12,4},{14,6},{1,9},{3,11}... | collective-permute-start | bytes 208904 | tf_op jit(solution)/shard_map/ppermute | solution.py:620
  17.1 2.3 %collective-permute-start.4 = (bf16[272,128]{1,0:T(8,128)(2,1)S(1)}, bf16[272,128]{1,0:T(8,128)(2,1)S(1)}, u32[]{:S(2)}, u32[]{:S(2)}) collective-permute-start(bf16[272,128]{1,0:T(8,128)(2,1)S(1)} %get-tuple-element.20), channel_id=1, source_target_pairs={{0,6},{2,4},{4,2},{6,0},{8,14},{10,12},{12,10},{14,8},{1,7},{3,5},... | collective-permute-start | bytes 208904 | tf_op jit(solution)/shard_map/ppermute | solution.py:620
  19.4 0.0 collective-permute-done.after_ref.rest_2_
  19.4 1.3 %collective-permute-start.5 = (bf16[272,128]{1,0:T(8,128)(2,1)S(1)}, bf16[272,128]{1,0:T(8,128)(2,1)S(1)}, u32[]{:S(2)}, u32[]{:S(2)}) collective-permute-start(bf16[272,128]{1,0:T(8,128)(2,1)S(1)} %get-tuple-element.21), channel_id=1, source_target_pairs={{0,4},{2,6},{4,0},{6,2},{8,12},{10,14},{12,8},{14,10},{1,5},{3,7},... | collective-permute-start | bytes 208904 | tf_op jit(solution)/shard_map/ppermute | solution.py:620
  20.8 0.0 collective-permute-done.1.rest_1_
  20.8 1.2 %collective-permute-start.6 = (bf16[272,128]{1,0:T(8,128)(2,1)S(1)}, bf16[272,128]{1,0:T(8,128)(2,1)S(1)}, u32[]{:S(2)}, u32[]{:S(2)}) collective-permute-start(bf16[272,128]{1,0:T(8,128)(2,1)S(1)} %get-tuple-element.22), channel_id=1, source_target_pairs={{0,2},{2,0},{4,6},{6,4},{8,10},{10,8},{12,14},{14,12},{1,3},{3,1},... | collective-permute-start | bytes 208904 | tf_op jit(solution)/shard_map/ppermute | solution.py:620
  22.0 0.0 copy-done.4
  22.0 0.5 %fine_taps.1.taps_ref = f32[2168,128]{1,0:T(8,128)S(1)} custom-call(f32[5,3456]{1,0:T(8,128)S(1)} %copy-done.4, bf16[272,128]{1,0:T(8,128)(2,1)S(1)} %collective-permute-done.after_ref.rest_2_), custom_call_target="tpu_custom_call" | custom-call | tf_op jit(solution)/shard_map/fine_taps/pallas_call | solution.py:624
  22.4 2.5 %collective-permute-done.2.rest_3_ = bf16[272,128]{1,0:T(8,128)(2,1)S(1)} collective-permute-done((bf16[272,128]{1,0:T(8,128)(2,1)S(1)}, bf16[272,128]{1,0:T(8,128)(2,1)S(1)}, u32[]{:S(2)}, u32[]{:S(2)}) %collective-permute-start.2) | collective-permute-done | bytes 69664 | tf_op jit(solution)/shard_map/ppermute | solution.py:620
  24.9 0.2 collective-permute-done.3.rest_4_
  25.1 0.1 merge.1.kept_ref
  25.3 0.0 collective-permute-done.4.rest_0_
  25.3 0.5 %collective-permute-done.5.rest_1_ = bf16[272,128]{1,0:T(8,128)(2,1)S(1)} collective-permute-done((bf16[272,128]{1,0:T(8,128)(2,1)S(1)}, bf16[272,128]{1,0:T(8,128)(2,1)S(1)}, u32[]{:S(2)}, u32[]{:S(2)}) %collective-permute-start.5) | collective-permute-done | bytes 69664 | tf_op jit(solution)/shard_map/ppermute | solution.py:620
  25.8 0.0 collective-permute-done.6.rest_2_
  25.8 0.0 copy-done.3
  25.8 0.0 copy-done.1
  25.8 0.0 copy-done.2
  25.8 0.0 copy-done
  25.8 1.7 %section_two.1 = f32[2,1,14580]{2,1,0:T(1,128)} custom-call(s32[8,128]{1,0:T(8,128)S(1)} %get-tuple-element.14.width_ref, f32[432,128]{1,0:T(8,128)S(1)} %merge.1.kept_ref, f32[2168,128]{1,0:T(8,128)S(1)} %fine_taps.1.taps_ref, bf16[432,1024]{1,0:T(8,128)(2,1)S(1)} %copy-done, f32[128,512]{1,0:T(8,128)S(1)} %copy-done.2, f32[128,512]{1,0:T(8,128)S(1)} %copy-done.1, ...), custom_call_target="tpu_custom_call" | custom-call | tf_op jit(solution)/shard_map/section_two/pallas_call | solution.py:643
  (4 shorter events, 0.0 us)
Async XLA Ops:
  0.0 25.8 %copy-start.3 = (bf16[128,512]{1,0:T(8,128)(2,1)S(1)}, bf16[128,512]{1,0:T(8,128)(2,1)}, u32[]{:S(2)}) copy-start(bf16[128,512]{1,0:T(8,128)(2,1)} %constant.11.clone.join_ref) | copy-start | bytes 393220
  0.0 25.8 %copy-start.1 = (f32[128,512]{1,0:T(8,128)S(1)}, f32[128,512]{1,0:T(8,128)}, u32[]{:S(2)}) copy-start(f32[128,512]{1,0:T(8,128)} %constant.10.clone.sin_ref) | copy-start | bytes 786436
  0.0 25.8 %copy-start.2 = (f32[128,512]{1,0:T(8,128)S(1)}, f32[128,512]{1,0:T(8,128)}, u32[]{:S(2)}) copy-start(f32[128,512]{1,0:T(8,128)} %constant.9.clone.cos_ref) | copy-start | bytes 786436
  0.0 25.8 %copy-start = (bf16[432,1024]{1,0:T(8,128)(2,1)S(1)}, bf16[432,1024]{1,0:T(8,128)(2,1)}, u32[]{:S(2)}) copy-start(bf16[432,1024]{1,0:T(8,128)(2,1)} %constant.8.clone.dft_ref) | copy-start | bytes 2654212
  0.0 22.0 %copy-start.4 = (f32[5,3456]{1,0:T(8,128)S(1)}, f32[5,3456]{1,0:T(8,128)}, u32[]{:S(2)}) copy-start(f32[5,3456]{1,0:T(8,128)} %taps_ref.1) | copy-start | bytes 207364
  8.1 11.4 %collective-permute-start = (bf16[272,128]{1,0:T(8,128)(2,1)S(1)}, bf16[272,128]{1,0:T(8,128)(2,1)S(1)}, u32[]{:S(2)}, u32[]{:S(2)}) collective-permute-start(bf16[272,128]{1,0:T(8,128)(2,1)S(1)} %get-tuple-element.15), channel_id=1, source_target_pairs={{0,12},{2,14},{4,8},{6,10},{8,4},{10,6},{12,0},{14,2},{1,13},{3,15... | collective-permute-start | bytes 208904 | tf_op jit(solution)/shard_map/ppermute | solution.py:620
  13.2 7.6 %collective-permute-start.1 = (bf16[272,128]{1,0:T(8,128)(2,1)S(1)}, bf16[272,128]{1,0:T(8,128)(2,1)S(1)}, u32[]{:S(2)}, u32[]{:S(2)}) collective-permute-start(bf16[272,128]{1,0:T(8,128)(2,1)S(1)} %get-tuple-element.17), channel_id=1, source_target_pairs={{0,14},{2,12},{4,10},{6,8},{8,6},{10,4},{12,2},{14,0},{1,15},{3,13... | collective-permute-start | bytes 208904 | tf_op jit(solution)/shard_map/ppermute | solution.py:620
  14.3 10.6 %collective-permute-start.2 = (bf16[272,128]{1,0:T(8,128)(2,1)S(1)}, bf16[272,128]{1,0:T(8,128)(2,1)S(1)}, u32[]{:S(2)}, u32[]{:S(2)}) collective-permute-start(bf16[272,128]{1,0:T(8,128)(2,1)S(1)} %get-tuple-element.18), channel_id=1, source_target_pairs={{0,10},{2,8},{4,14},{6,12},{8,2},{10,0},{12,6},{14,4},{1,11},{3,9}... | collective-permute-start | bytes 208904 | tf_op jit(solution)/shard_map/ppermute | solution.py:620
  15.1 10.0 %collective-permute-start.3 = (bf16[272,128]{1,0:T(8,128)(2,1)S(1)}, bf16[272,128]{1,0:T(8,128)(2,1)S(1)}, u32[]{:S(2)}, u32[]{:S(2)}) collective-permute-start(bf16[272,128]{1,0:T(8,128)(2,1)S(1)} %get-tuple-element.19), channel_id=1, source_target_pairs={{0,8},{2,10},{4,12},{6,14},{8,0},{10,2},{12,4},{14,6},{1,9},{3,11}... | collective-permute-start | bytes 208904 | tf_op jit(solution)/shard_map/ppermute | solution.py:620
  17.1 8.2 %collective-permute-start.4 = (bf16[272,128]{1,0:T(8,128)(2,1)S(1)}, bf16[272,128]{1,0:T(8,128)(2,1)S(1)}, u32[]{:S(2)}, u32[]{:S(2)}) collective-permute-start(bf16[272,128]{1,0:T(8,128)(2,1)S(1)} %get-tuple-element.20), channel_id=1, source_target_pairs={{0,6},{2,4},{4,2},{6,0},{8,14},{10,12},{12,10},{14,8},{1,7},{3,5},... | collective-permute-start | bytes 208904 | tf_op jit(solution)/shard_map/ppermute | solution.py:620
  19.4 6.3 %collective-permute-start.5 = (bf16[272,128]{1,0:T(8,128)(2,1)S(1)}, bf16[272,128]{1,0:T(8,128)(2,1)S(1)}, u32[]{:S(2)}, u32[]{:S(2)}) collective-permute-start(bf16[272,128]{1,0:T(8,128)(2,1)S(1)} %get-tuple-element.21), channel_id=1, source_target_pairs={{0,4},{2,6},{4,0},{6,2},{8,12},{10,14},{12,8},{14,10},{1,5},{3,7},... | collective-permute-start | bytes 208904 | tf_op jit(solution)/shard_map/ppermute | solution.py:620
  20.8 5.0 %collective-permute-start.6 = (bf16[272,128]{1,0:T(8,128)(2,1)S(1)}, bf16[272,128]{1,0:T(8,128)(2,1)S(1)}, u32[]{:S(2)}, u32[]{:S(2)}) collective-permute-start(bf16[272,128]{1,0:T(8,128)(2,1)S(1)} %get-tuple-element.22), channel_id=1, source_target_pairs={{0,2},{2,0},{4,6},{6,4},{8,10},{10,8},{12,14},{14,12},{1,3},{3,1},... | collective-permute-start | bytes 208904 | tf_op jit(solution)/shard_map/ppermute | solution.py:620

commit v7 on v6

--- a/solution.py
+++ b/solution.py
@@ -284,7 +284,7 @@
     acc = jnp.zeros((count, columns), jnp.float32)
     order = sorted(range(plan.depth // LANES), key=lambda index: (index % blocks, index // blocks))
     turns = chan_len // LANES
-    bounds = (9, blocks)
+    bounds = (5, 12, blocks)
 
     def column_tile(index):
         scale = jnp.concatenate(
@@ -493,17 +493,15 @@
         count = after - first + 1
         for part in range(2):
             picked = part * slots + place + 1
-            tiles = []
-            for tile in range(count):
-                value = parts[tile + 1][part * slots : (part + 1) * slots]
-                if offset:
-                    before = parts[tile][part * slots : (part + 1) * slots]
-                    value = jnp.where(
-                        lane[:slots] < offset,
-                        pltpu.roll(before, offset, axis=1),
-                        pltpu.roll(value, offset, axis=1),
-                    )
-                tiles.append(value[picked % slots : picked % slots + 1])
+            pieces = [value[part * slots : (part + 1) * slots] for value in parts[: count + 1]]
+            if offset:
+                turned = [pltpu.roll(value, offset, axis=1) for value in pieces]
+                pieces = [None] + [
+                    jnp.where(lane[:slots] < offset, before, value)
+                    for before, value in zip(turned, turned[1:])
+                ]
+            row_of = picked % slots
+            tiles = [value[row_of : row_of + 1] for value in pieces[1:]]
             if place:
                 tiles[0] = tiles[0] + carry[part]
             carry[part] = tiles[-1]

time: 27.8 us -> 27.8 us (level)
  no operation moved by 1% of the time
where the time goes in v7:
time: 27.8 us; the launch traced here: 27.5 us
  starting transfers between devices  13.9 us (50%)
  Pallas kernels  10.3 us (37%)
  waiting for transfers between devices  3.17 us (11%)
    ppermute x7, starting transfers between devices, direct_plan(): received[step] = lax.ppermute(sent[step], ('tm', 'zoom'), pairs)  13.9 us
    pallas_call x1, Pallas kernels, direct_plan(): pl.pallas_call(functools.partial(section_one_kernel, plan), out_shape=[bl...  8.05 us
    ppermute x7, waiting for transfers between devices, direct_plan(): received[step] = lax.ppermute(sent[step], ('tm', 'zoom'), pairs)  3.17 us
    pallas_call x1, Pallas kernels, direct_plan(): pl.pallas_call(functools.partial(section_two_kernel, plan, late), out_sha...  1.65 us
  transfers between devices with their start and end apart: 7, of which 3 were waited for; matrix products, arithmetic and copies ran while one was open for 0% of the time, Pallas kernels for 2%

profile of v7, /device:TPU:0, one launch (start us, length us, event | category | flops | bytes accessed | tf_op | source)
XLA Modules:
  0.0 27.5 jit_solution(17038909124768829281)
XLA Ops:
  0.0 0.0 copy-start.3
  0.0 8.1 %section_one.1 = (bf16[272,128]{1,0:T(8,128)(2,1)S(1)}, bf16[272,128]{1,0:T(8,128)(2,1)S(1)}, bf16[272,128]{1,0:T(8,128)(2,1)S(1)}, bf16[272,128]{1,0:T(8,128)(2...) custom-call(s32[2]{0:T(128)} %starts_hbm.1, ...), custom_call_target="tpu_custom_call" | custom-call | tf_op jit(solution)/shard_map/section_one/pallas_call | solution.py:596
  8.1 5.1 %collective-permute-start = (bf16[272,128]{1,0:T(8,128)(2,1)S(1)}, bf16[272,128]{1,0:T(8,128)(2,1)S(1)}, u32[]{:S(2)}, u32[]{:S(2)}) collective-permute-start(bf16[272,128]{1,0:T(8,128)(2,1)S(1)} %get-tuple-element.15), channel_id=1, source_target_pairs={{0,12},{2,14},{4,8},{6,10},{8,4},{10,6},{12,0},{14,2},{1,13},{3,15... | collective-permute-start | bytes 208904 | tf_op jit(solution)/shard_map/ppermute | solution.py:618
  13.2 1.1 %collective-permute-start.1 = (bf16[272,128]{1,0:T(8,128)(2,1)S(1)}, bf16[272,128]{1,0:T(8,128)(2,1)S(1)}, u32[]{:S(2)}, u32[]{:S(2)}) collective-permute-start(bf16[272,128]{1,0:T(8,128)(2,1)S(1)} %get-tuple-element.17), channel_id=1, source_target_pairs={{0,14},{2,12},{4,10},{6,8},{8,6},{10,4},{12,2},{14,0},{1,15},{3,13... | collective-permute-start | bytes 208904 | tf_op jit(solution)/shard_map/ppermute | solution.py:618
  14.4 0.8 %collective-permute-start.2 = (bf16[272,128]{1,0:T(8,128)(2,1)S(1)}, bf16[272,128]{1,0:T(8,128)(2,1)S(1)}, u32[]{:S(2)}, u32[]{:S(2)}) collective-permute-start(bf16[272,128]{1,0:T(8,128)(2,1)S(1)} %get-tuple-element.18), channel_id=1, source_target_pairs={{0,10},{2,8},{4,14},{6,12},{8,2},{10,0},{12,6},{14,4},{1,11},{3,9}... | collective-permute-start | bytes 208904 | tf_op jit(solution)/shard_map/ppermute | solution.py:618
  15.1 2.0 %collective-permute-start.3 = (bf16[272,128]{1,0:T(8,128)(2,1)S(1)}, bf16[272,128]{1,0:T(8,128)(2,1)S(1)}, u32[]{:S(2)}, u32[]{:S(2)}) collective-permute-start(bf16[272,128]{1,0:T(8,128)(2,1)S(1)} %get-tuple-element.19), channel_id=1, source_target_pairs={{0,8},{2,10},{4,12},{6,14},{8,0},{10,2},{12,4},{14,6},{1,9},{3,11}... | collective-permute-start | bytes 208904 | tf_op jit(solution)/shard_map/ppermute | solution.py:618
  17.1 2.3 %collective-permute-start.4 = (bf16[272,128]{1,0:T(8,128)(2,1)S(1)}, bf16[272,128]{1,0:T(8,128)(2,1)S(1)}, u32[]{:S(2)}, u32[]{:S(2)}) collective-permute-start(bf16[272,128]{1,0:T(8,128)(2,1)S(1)} %get-tuple-element.20), channel_id=1, source_target_pairs={{0,6},{2,4},{4,2},{6,0},{8,14},{10,12},{12,10},{14,8},{1,7},{3,5},... | collective-permute-start | bytes 208904 | tf_op jit(solution)/shard_map/ppermute | solution.py:618
  19.4 0.0 collective-permute-done.after_ref.rest_2_
  19.4 1.3 %collective-permute-start.5 = (bf16[272,128]{1,0:T(8,128)(2,1)S(1)}, bf16[272,128]{1,0:T(8,128)(2,1)S(1)}, u32[]{:S(2)}, u32[]{:S(2)}) collective-permute-start(bf16[272,128]{1,0:T(8,128)(2,1)S(1)} %get-tuple-element.21), channel_id=1, source_target_pairs={{0,4},{2,6},{4,0},{6,2},{8,12},{10,14},{12,8},{14,10},{1,5},{3,7},... | collective-permute-start | bytes 208904 | tf_op jit(solution)/shard_map/ppermute | solution.py:618
  20.7 0.0 collective-permute-done.1.rest_1_
  20.7 1.2 %collective-permute-start.6 = (bf16[272,128]{1,0:T(8,128)(2,1)S(1)}, bf16[272,128]{1,0:T(8,128)(2,1)S(1)}, u32[]{:S(2)}, u32[]{:S(2)}) collective-permute-start(bf16[272,128]{1,0:T(8,128)(2,1)S(1)} %get-tuple-element.22), channel_id=1, source_target_pairs={{0,2},{2,0},{4,6},{6,4},{8,10},{10,8},{12,14},{14,12},{1,3},{3,1},... | collective-permute-start | bytes 208904 | tf_op jit(solution)/shard_map/ppermute | solution.py:618
  22.0 0.0 copy-done.4
  22.0 0.5 %fine_taps.1.taps_ref = f32[2168,128]{1,0:T(8,128)S(1)} custom-call(f32[5,3456]{1,0:T(8,128)S(1)} %copy-done.4, bf16[272,128]{1,0:T(8,128)(2,1)S(1)} %collective-permute-done.after_ref.rest_2_), custom_call_target="tpu_custom_call" | custom-call | tf_op jit(solution)/shard_map/fine_taps/pallas_call | solution.py:622
  22.5 2.5 %collective-permute-done.2.rest_3_ = bf16[272,128]{1,0:T(8,128)(2,1)S(1)} collective-permute-done((bf16[272,128]{1,0:T(8,128)(2,1)S(1)}, bf16[272,128]{1,0:T(8,128)(2,1)S(1)}, u32[]{:S(2)}, u32[]{:S(2)}) %collective-permute-start.2) | collective-permute-done | bytes 69664 | tf_op jit(solution)/shard_map/ppermute | solution.py:618
  25.0 0.2 collective-permute-done.3.rest_4_
  25.1 0.1 merge.1.kept_ref
  25.3 0.0 collective-permute-done.4.rest_0_
  25.3 0.5 %collective-permute-done.5.rest_1_ = bf16[272,128]{1,0:T(8,128)(2,1)S(1)} collective-permute-done((bf16[272,128]{1,0:T(8,128)(2,1)S(1)}, bf16[272,128]{1,0:T(8,128)(2,1)S(1)}, u32[]{:S(2)}, u32[]{:S(2)}) %collective-permute-start.5) | collective-permute-done | bytes 69664 | tf_op jit(solution)/shard_map/ppermute | solution.py:618
  25.8 0.0 collective-permute-done.6.rest_2_
  25.8 0.0 copy-done.3
  25.8 0.0 copy-done.1
  25.8 0.0 copy-done.2
  25.8 0.0 copy-done
  25.8 1.6 %section_two.1 = f32[2,1,14580]{2,1,0:T(1,128)} custom-call(s32[8,128]{1,0:T(8,128)S(1)} %get-tuple-element.14.width_ref, f32[432,128]{1,0:T(8,128)S(1)} %merge.1.kept_ref, f32[2168,128]{1,0:T(8,128)S(1)} %fine_taps.1.taps_ref, bf16[432,1024]{1,0:T(8,128)(2,1)S(1)} %copy-done, f32[128,512]{1,0:T(8,128)S(1)} %copy-done.2, f32[128,512]{1,0:T(8,128)S(1)} %copy-done.1, ...), custom_call_target="tpu_custom_call" | custom-call | tf_op jit(solution)/shard_map/section_two/pallas_call | solution.py:641
  (4 shorter events, 0.0 us)
Async XLA Ops:
  0.0 25.8 %copy-start.3 = (bf16[128,512]{1,0:T(8,128)(2,1)S(1)}, bf16[128,512]{1,0:T(8,128)(2,1)}, u32[]{:S(2)}) copy-start(bf16[128,512]{1,0:T(8,128)(2,1)} %constant.11.clone.join_ref) | copy-start | bytes 393220
  0.0 25.8 %copy-start.1 = (f32[128,512]{1,0:T(8,128)S(1)}, f32[128,512]{1,0:T(8,128)}, u32[]{:S(2)}) copy-start(f32[128,512]{1,0:T(8,128)} %constant.10.clone.sin_ref) | copy-start | bytes 786436
  0.0 25.8 %copy-start.2 = (f32[128,512]{1,0:T(8,128)S(1)}, f32[128,512]{1,0:T(8,128)}, u32[]{:S(2)}) copy-start(f32[128,512]{1,0:T(8,128)} %constant.9.clone.cos_ref) | copy-start | bytes 786436
  0.0 25.8 %copy-start = (bf16[432,1024]{1,0:T(8,128)(2,1)S(1)}, bf16[432,1024]{1,0:T(8,128)(2,1)}, u32[]{:S(2)}) copy-start(bf16[432,1024]{1,0:T(8,128)(2,1)} %constant.8.clone.dft_ref) | copy-start | bytes 2654212
  0.0 22.0 %copy-start.4 = (f32[5,3456]{1,0:T(8,128)S(1)}, f32[5,3456]{1,0:T(8,128)}, u32[]{:S(2)}) copy-start(f32[5,3456]{1,0:T(8,128)} %taps_ref.1) | copy-start | bytes 207364
  8.1 11.4 %collective-permute-start = (bf16[272,128]{1,0:T(8,128)(2,1)S(1)}, bf16[272,128]{1,0:T(8,128)(2,1)S(1)}, u32[]{:S(2)}, u32[]{:S(2)}) collective-permute-start(bf16[272,128]{1,0:T(8,128)(2,1)S(1)} %get-tuple-element.15), channel_id=1, source_target_pairs={{0,12},{2,14},{4,8},{6,10},{8,4},{10,6},{12,0},{14,2},{1,13},{3,15... | collective-permute-start | bytes 208904 | tf_op jit(solution)/shard_map/ppermute | solution.py:618
  13.2 7.5 %collective-permute-start.1 = (bf16[272,128]{1,0:T(8,128)(2,1)S(1)}, bf16[272,128]{1,0:T(8,128)(2,1)S(1)}, u32[]{:S(2)}, u32[]{:S(2)}) collective-permute-start(bf16[272,128]{1,0:T(8,128)(2,1)S(1)} %get-tuple-element.17), channel_id=1, source_target_pairs={{0,14},{2,12},{4,10},{6,8},{8,6},{10,4},{12,2},{14,0},{1,15},{3,13... | collective-permute-start | bytes 208904 | tf_op jit(solution)/shard_map/ppermute | solution.py:618
  14.4 10.6 %collective-permute-start.2 = (bf16[272,128]{1,0:T(8,128)(2,1)S(1)}, bf16[272,128]{1,0:T(8,128)(2,1)S(1)}, u32[]{:S(2)}, u32[]{:S(2)}) collective-permute-start(bf16[272,128]{1,0:T(8,128)(2,1)S(1)} %get-tuple-element.18), channel_id=1, source_target_pairs={{0,10},{2,8},{4,14},{6,12},{8,2},{10,0},{12,6},{14,4},{1,11},{3,9}... | collective-permute-start | bytes 208904 | tf_op jit(solution)/shard_map/ppermute | solution.py:618
  15.1 10.0 %collective-permute-start.3 = (bf16[272,128]{1,0:T(8,128)(2,1)S(1)}, bf16[272,128]{1,0:T(8,128)(2,1)S(1)}, u32[]{:S(2)}, u32[]{:S(2)}) collective-permute-start(bf16[272,128]{1,0:T(8,128)(2,1)S(1)} %get-tuple-element.19), channel_id=1, source_target_pairs={{0,8},{2,10},{4,12},{6,14},{8,0},{10,2},{12,4},{14,6},{1,9},{3,11}... | collective-permute-start | bytes 208904 | tf_op jit(solution)/shard_map/ppermute | solution.py:618
  17.1 8.2 %collective-permute-start.4 = (bf16[272,128]{1,0:T(8,128)(2,1)S(1)}, bf16[272,128]{1,0:T(8,128)(2,1)S(1)}, u32[]{:S(2)}, u32[]{:S(2)}) collective-permute-start(bf16[272,128]{1,0:T(8,128)(2,1)S(1)} %get-tuple-element.20), channel_id=1, source_target_pairs={{0,6},{2,4},{4,2},{6,0},{8,14},{10,12},{12,10},{14,8},{1,7},{3,5},... | collective-permute-start | bytes 208904 | tf_op jit(solution)/shard_map/ppermute | solution.py:618
  19.4 6.3 %collective-permute-start.5 = (bf16[272,128]{1,0:T(8,128)(2,1)S(1)}, bf16[272,128]{1,0:T(8,128)(2,1)S(1)}, u32[]{:S(2)}, u32[]{:S(2)}) collective-permute-start(bf16[272,128]{1,0:T(8,128)(2,1)S(1)} %get-tuple-element.21), channel_id=1, source_target_pairs={{0,4},{2,6},{4,0},{6,2},{8,12},{10,14},{12,8},{14,10},{1,5},{3,7},... | collective-permute-start | bytes 208904 | tf_op jit(solution)/shard_map/ppermute | solution.py:618
  20.7 5.0 %collective-permute-start.6 = (bf16[272,128]{1,0:T(8,128)(2,1)S(1)}, bf16[272,128]{1,0:T(8,128)(2,1)S(1)}, u32[]{:S(2)}, u32[]{:S(2)}) collective-permute-start(bf16[272,128]{1,0:T(8,128)(2,1)S(1)} %get-tuple-element.22), channel_id=1, source_target_pairs={{0,2},{2,0},{4,6},{6,4},{8,10},{10,8},{12,14},{14,12},{1,3},{3,1},... | collective-permute-start | bytes 208904 | tf_op jit(solution)/shard_map/ppermute | solution.py:618
